TPU v7x, 256 devices: a whole 4x4x8 slice. The times are simulated.
256 devices in a mesh: chain: 32 (over z, x), sector: 8 (over y, core).
Axes of the slice: x: 4, y: 4, z: 8, core: 2. Of those that a mesh axis runs over, the one named last changes fastest.
Arguments:
- wave_start: float32 [32, 16, 128, 16, 128], P('chain', 'sector'), may hold values from -6 to 6
- transfer: float32 [32, 16, 128, 128], P('chain', 'sector'), as said below
- energy_terms: float32 [32, 16, 128, 128], P('chain', 'sector'), may hold values from -1.5 to 1.5
- coupling: float32 [32, 16, 128, 128], P('chain', 'sector'), may hold values from -0.5 to 0.5
- physical: float32 [32, 16, 16], P('chain'), may hold values from -6 to 6
- kept_ranks: int32 [32, 16], P('chain', 'sector'), may hold values from 32 to 128
Outputs:
- wave_kept: float32 [32, 16, 128, 16, 128], P('chain', 'sector')
- energy: float32 [32], P('chain')
- left_env: float32 [32, 16, 128, 128], P('chain', 'sector')
Inputs may be any that keep to these rules, and one draw needn't show every extreme that they name: `kept_ranks`: kept bond states of a sector, at most 128. Each sector's transfer matrix has a dominant positive diagonal and small off-diagonal entries.
All inputs are finite; a program needn't handle non-finite values.
Results may differ from a plain program's by a relative error of at most 0.0003.
Values sent between devices are 32-bit elements; how exact they have to be, the bound alone decides.
A program may use at most 128 MiB of HBM per device.

v0:
```python
import jax
import jax.numpy as jnp
from jax import lax
from jax.sharding import PartitionSpec as P

ITERS = 2


HIGHEST = lax.Precision.HIGHEST
EPS = 1e-06


def shifted(block, axis, distance):
    devices = range(lax.axis_size(axis))
    route = [(i - distance, i) for i in devices if i - distance in devices]
    return lax.ppermute(block, axis, route)


def symmetric(matrix):
    return 0.5 * (matrix + jnp.swapaxes(matrix, -1, -2))


def local_terms(wave, left_blk, right_blk, sym_phys):
    result = jnp.einsum("kab,kbpc->kapc", left_blk, wave, precision=HIGHEST)
    result = result + jnp.einsum("kapb,kbc->kapc", wave, right_blk, precision=HIGHEST)
    return result + jnp.einsum("pq,kaqc->kapc", sym_phys, wave, precision=HIGHEST)


def apply_products(wave, left_blk, right_blk, sym_phys, coupler):
    result = local_terms(wave, left_blk, right_blk, sym_phys)
    raised = jnp.einsum("kab,kbpc->kapc", coupler, wave, precision=HIGHEST)
    from_below = shifted(raised[-1:], "sector", 1)
    from_above = shifted(wave[:1], "sector", -1)
    incoming = jnp.concatenate([from_below, raised[:-1]], axis=0)
    above = jnp.concatenate([wave[1:], from_above], axis=0)
    lowered = jnp.einsum("kba,kbpc->kapc", coupler, above, precision=HIGHEST)
    return result + incoming + lowered


def per_device(wave_start, transfer, energy_terms, coupling, physical, kept_ranks):
    sources = symmetric(energy_terms)
    zero_env = jnp.zeros_like(transfer)

    def advance(turn_index, carry):
        left_now, right_now = carry
        left_out = (
            jnp.einsum("...ji,...jl,...lm->...im", transfer, left_now, transfer, precision=HIGHEST)
            + sources
        )
        right_out = (
            jnp.einsum("...ij,...jl,...ml->...im", transfer, right_now, transfer, precision=HIGHEST)
            + sources
        )
        left_next = shifted(left_out, "chain", 1)
        right_next = shifted(right_out, "chain", -1)
        return (left_next, right_next)

    left_env, right_env = lax.fori_loop(
        0, lax.axis_size("chain") - 1, advance, (zero_env, zero_env)
    )
    left_blk = left_env[0]
    right_blk = right_env[0]
    sym_phys = symmetric(physical[0])
    coupler = coupling[0]

    def operate(vector):
        return apply_products(vector, left_blk, right_blk, sym_phys, coupler)

    wave = wave_start[0]
    norm_start = lax.psum(jnp.sum(wave * wave), "sector")
    wave = wave / jnp.sqrt(norm_start)
    applied = operate(wave)
    energy = jnp.float32(0.0)
    for iteration in range(ITERS):
        correlation = lax.psum(jnp.sum(wave * applied), "sector")
        residual = applied - correlation * wave
        res_norm = lax.psum(jnp.sum(residual * residual), "sector")
        unit_dir = residual / jnp.sqrt(res_norm + EPS)
        turned = operate(unit_dir)
        curvature, coupled = lax.psum(
            (jnp.sum(unit_dir * turned), jnp.sum(applied * unit_dir)), "sector"
        )
        energy = 0.5 * (correlation + curvature) - jnp.sqrt(
            0.25 * (correlation - curvature) ** 2 + coupled * coupled
        )
        coef_new = energy - correlation
        magnitude = jnp.sqrt(coupled * coupled + coef_new * coef_new)
        wave = (coupled * wave + coef_new * unit_dir) / magnitude
        applied = (coupled * applied + coef_new * turned) / magnitude
    columns = lax.broadcasted_iota(jnp.int32, (1, 1, 1, wave.shape[-1]), 3)
    kept_mask = (columns < kept_ranks[0][:, None, None, None]).astype(wave.dtype)
    truncated = wave * kept_mask
    kept_total = lax.psum(jnp.sum(truncated * truncated), "sector")
    truncated = truncated / jnp.sqrt(kept_total + EPS)
    return (truncated[None], jnp.reshape(energy, (1,)), left_env)


def solution(mesh):
    placed = (
        P("chain", "sector", None, None, None),
        P("chain", "sector", None, None),
        P("chain", "sector", None, None),
        P("chain", "sector", None, None),
        P("chain", None, None),
        P("chain", "sector"),
    )
    return jax.shard_map(
        per_device,
        mesh=mesh,
        in_specs=placed,
        out_specs=(
            P("chain", "sector", None, None, None),
            P("chain"),
            P("chain", "sector", None, None),
        ),
        check_vma=False,
    )
```

profile of v0, /device:TPU:103, one launch (start us, length us, event | category | flops | bytes accessed | tf_op | source)
XLA Modules:
  0.0 661.1 jit_solution(10697075020741569792)
XLA Ops:
  3.5 13.2 %psum.70 = f32[]{:T(128)} all-reduce(f32[]{:T(128)} %multiply_reduce_fusion.8), channel_id=1, replica_groups=mesh['chain'=32,'sector'=8] {'sector'}, use_global_device_ids=true, to_apply=%region_3.0 | all-reduce | flops 1 | bytes 8 | tf_op jit(solution)/shard_map/psum | solution.py:70
  32.7 5.9 fusion.31
  38.6 390.6 %while.12 = (s32[]{:T(128)}, f32[1,2,128,128]{3,2,1,0:T(8,128)S(1)}, f32[1,2,128,128]{3,2,1,0:T(8,128)S(1)}, f32[1,2,128,128]{3,2,1,0:T(8,128)S(1)}, f32[1,2,128,128]{3,2,1,0:T(8,128)S(1)}, /*index=5*/s32[]{:T(128)}) while((s32[]{:T(128)}, f32[1,2,128,128]{3,2,1,0:T(8,128)S(1)}, f32[1,2,128,128]{3,2,1,0:T(8,128)S(1)}, ...), condition=%wide.region_1.0_spmd, body=%wide.region_0.0_spmd.sunk | while | flops 201392128 | bytes 2883733 | solution.py:58
  47.2 8.1 %collective-permute-done.1 = f32[1,2,128,128]{3,2,1,0:T(8,128)S(1)} collective-permute-done((f32[1,2,128,128]{3,2,1,0:T(8,128)S(1)}, f32[1,2,128,128]{3,2,1,0:T(8,128)S(1)}, u32[]{:S(2)}, u32[]{:S(2)}) %collective-permute-start.1) | collective-permute-done | bytes 131104 | tf_op jit(solution)/shard_map/while/body/eval_jaxpr/ppermute | solution.py:16
  62.4 5.9 collective-permute-done.1
  74.9 5.7 collective-permute-done.1
  87.2 5.6 collective-permute-done.1
  185.5 5.8 collective-permute-done.1
  199.2 5.9 collective-permute-done.1
  212.3 5.9 collective-permute-done.1
  224.9 5.6 collective-permute-done.1
  335.4 5.7 collective-permute-done.1
  348.7 5.9 collective-permute-done.1
  361.8 5.9 collective-permute-done.1
  374.4 5.6 collective-permute-done.1
  435.0 6.6 %multiply_reduce_fusion.7 = (f32[]{:T(128)}, f32[2,128,16,128]{3,1,2,0:T(8,128)}) fusion(f32[1,2,128,16,128]{4,2,3,1,0:T(8,128)S(1)} %copy-done.3, f32[1,2,128,128]{3,2,1,0:T(8,128)S(1)} %copy-done, f32[1,128,16,128]{3,1,2,0:T(8,128)} %collective-permute-done.3, f32[1,128,16,128]{3,1,2,0:T(8,128)S(1)} %copy-done.8, f32[1,128,16,128]{3,1,2,0:T(8,128)S(1)} %copy-done.7, ...), kind=kOutput, calls=%fused_computation.55 | convolution fusion | flops 809500672 | bytes 14811140 | tf_op jit(solution)/shard_map/kba,kbpc->kapc/dot_general | solution.py:36
  441.6 46.7 %psum.71 = f32[]{:T(128)} all-reduce(f32[]{:T(128)} %get-tuple-element.69), channel_id=1, replica_groups=mesh['chain'=32,'sector'=8] {'sector'}, use_global_device_ids=true, to_apply=%region_5.0 | all-reduce | flops 1 | bytes 8 | tf_op jit(solution)/shard_map/psum | solution.py:75
  491.9 13.0 %psum.72 = f32[]{:T(128)} all-reduce(f32[]{:T(128)} %multiply_reduce_fusion.6), channel_id=1, replica_groups=mesh['chain'=32,'sector'=8] {'sector'}, use_global_device_ids=true, to_apply=%region_7.0 | all-reduce | flops 1 | bytes 8 | tf_op jit(solution)/shard_map/psum | solution.py:77
  535.2 10.1 %all-reduce.1 = (f32[]{:T(128)}, f32[]{:T(128)}) all-reduce(f32[]{:T(128)} %get-tuple-element.37, f32[]{:T(128)} %get-tuple-element.36), channel_id=1, replica_groups=mesh['chain'=32,'sector'=8] {'sector'}, use_global_device_ids=true, to_apply=%region_9.0 | all-reduce | flops 2 | bytes 16 | tf_op jit(solution)/shard_map/psum | solution.py:80
  549.9 7.2 %multiply_reduce_fusion.3 = (f32[]{:T(128)}, f32[2,128,16,128]{3,1,2,0:T(8,128)}, f32[2,128,16,128]{3,1,2,0:T(8,128)}) fusion(f32[]{:T(128)S(6)} %sqrt.27, f32[2,128,16,128]{3,1,2,0:T(8,128)S(1)} %broadcast_divide_fusion.1, f32[]{:T(128)S(6)} %sub.27, f32[]{:T(128)} %get-tuple-element.50, f32[2,128,16,128]{3,1,2,0:T(8,128)} %get-tuple-element.71, ...), kind=kLoop, calls=%fused_computation.48 | loop fusion | flops 5767167 | bytes 12582932 | tf_op jit(solution)/shard_map/reduce_sum | solution.py:75
  557.0 15.9 %psum.75 = f32[]{:T(128)} all-reduce(f32[]{:T(128)} %get-tuple-element.54), channel_id=1, replica_groups=mesh['chain'=32,'sector'=8] {'sector'}, use_global_device_ids=true, to_apply=%region_13.0 | all-reduce | flops 1 | bytes 8 | tf_op jit(solution)/shard_map/psum | solution.py:75
  576.9 13.2 %psum.76 = f32[]{:T(128)} all-reduce(f32[]{:T(128)} %multiply_reduce_fusion.2), channel_id=1, replica_groups=mesh['chain'=32,'sector'=8] {'sector'}, use_global_device_ids=true, to_apply=%region_15.0 | all-reduce | flops 1 | bytes 8 | tf_op jit(solution)/shard_map/psum | solution.py:77
  619.2 10.2 %all-reduce = (f32[]{:T(128)}, f32[]{:T(128)}) all-reduce(f32[]{:T(128)} %get-tuple-element.52, f32[]{:T(128)} %fusion.22), channel_id=1, replica_groups=mesh['chain'=32,'sector'=8] {'sector'}, use_global_device_ids=true, to_apply=%region_17.0 | all-reduce | flops 2 | bytes 16 | tf_op jit(solution)/shard_map/psum | solution.py:80
  637.3 15.9 %psum.79 = f32[]{:T(128)} all-reduce(f32[]{:T(128)} %multiply_reduce_fusion), channel_id=1, replica_groups=mesh['chain'=32,'sector'=8] {'sector'}, use_global_device_ids=true, to_apply=%region_21.0 | all-reduce | flops 1 | bytes 8 | tf_op jit(solution)/shard_map/psum | solution.py:93
  (308 shorter events, 415.8 us)
Async XLA Ops:
  21.7 413.1 %collective-permute-start.2 = (f32[1,128,16,128]{3,1,2,0:T(8,128)}, f32[1,128,16,128]{3,1,2,0:T(8,128)}, u32[]{:S(2)}, u32[]{:S(2)}) collective-permute-start(f32[1,128,16,128]{3,1,2,0:T(8,128)} %get-tuple-element.67), channel_id=1, source_target_pairs={{0,1},{1,2},{2,3},{3,4},{4,5},{5,6},{6,7},{8,9},{9,10},{10,11},{11... | collective-permute-start | bytes 3145736 | tf_op jit(solution)/shard_map/ppermute | solution.py:16
  26.1 408.7 %collective-permute-start.3 = (f32[1,128,16,128]{3,1,2,0:T(8,128)}, f32[1,128,16,128]{3,1,2,0:T(8,128)}, u32[]{:S(2)}, u32[]{:S(2)}) collective-permute-start(f32[1,128,16,128]{3,1,2,0:T(8,128)} %get-tuple-element.66), channel_id=1, source_target_pairs={{1,0},{2,1},{3,2},{4,3},{5,4},{6,5},{7,6},{9,8},{10,9},{11,10},{12... | collective-permute-start | bytes 3145736 | tf_op jit(solution)/shard_map/ppermute | solution.py:16
  44.7 10.6 %collective-permute-start.1 = (f32[1,2,128,128]{3,2,1,0:T(8,128)S(1)}, f32[1,2,128,128]{3,2,1,0:T(8,128)S(1)}, u32[]{:S(2)}, u32[]{:S(2)}) collective-permute-start(f32[1,2,128,128]{3,2,1,0:T(8,128)S(1)} %fusion.108), channel_id=1, source_target_pairs={{8,0},{16,8},{24,16},{32,24},{40,32},{48,40},{56,48},{64,56},{72,6... | collective-permute-start | bytes 393224 | tf_op jit(solution)/shard_map/while/body/eval_jaxpr/ppermute | solution.py:16
  58.5 9.7 %collective-permute-start.1 = (f32[1,2,128,128]{3,2,1,0:T(8,128)S(1)}, f32[1,2,128,128]{3,2,1,0:T(8,128)S(1)}, u32[]{:S(2)}, u32[]{:S(2)}) collective-permute-start(f32[1,2,128,128]{3,2,1,0:T(8,128)S(1)} %fusion.108), channel_id=1, source_target_pairs={{8,0},{16,8},{24,16},{32,24},{40,32},{48,40},{56,48},{64,56},{72,6... | collective-permute-start | bytes 393224 | tf_op jit(solution)/shard_map/while/body/eval_jaxpr/ppermute | solution.py:16
  83.8 9.0 %collective-permute-start.1 = (f32[1,2,128,128]{3,2,1,0:T(8,128)S(1)}, f32[1,2,128,128]{3,2,1,0:T(8,128)S(1)}, u32[]{:S(2)}, u32[]{:S(2)}) collective-permute-start(f32[1,2,128,128]{3,2,1,0:T(8,128)S(1)} %fusion.108), channel_id=1, source_target_pairs={{8,0},{16,8},{24,16},{32,24},{40,32},{48,40},{56,48},{64,56},{72,6... | collective-permute-start | bytes 393224 | tf_op jit(solution)/shard_map/while/body/eval_jaxpr/ppermute | solution.py:16
  96.1 9.0 %collective-permute-start.1 = (f32[1,2,128,128]{3,2,1,0:T(8,128)S(1)}, f32[1,2,128,128]{3,2,1,0:T(8,128)S(1)}, u32[]{:S(2)}, u32[]{:S(2)}) collective-permute-start(f32[1,2,128,128]{3,2,1,0:T(8,128)S(1)} %fusion.108), channel_id=1, source_target_pairs={{8,0},{16,8},{24,16},{32,24},{40,32},{48,40},{56,48},{64,56},{72,6... | collective-permute-start | bytes 393224 | tf_op jit(solution)/shard_map/while/body/eval_jaxpr/ppermute | solution.py:16
  108.4 9.0 %collective-permute-start.1 = (f32[1,2,128,128]{3,2,1,0:T(8,128)S(1)}, f32[1,2,128,128]{3,2,1,0:T(8,128)S(1)}, u32[]{:S(2)}, u32[]{:S(2)}) collective-permute-start(f32[1,2,128,128]{3,2,1,0:T(8,128)S(1)} %fusion.108), channel_id=1, source_target_pairs={{8,0},{16,8},{24,16},{32,24},{40,32},{48,40},{56,48},{64,56},{72,6... | collective-permute-start | bytes 393224 | tf_op jit(solution)/shard_map/while/body/eval_jaxpr/ppermute | solution.py:16
  157.5 9.0 %collective-permute-start.1 = (f32[1,2,128,128]{3,2,1,0:T(8,128)S(1)}, f32[1,2,128,128]{3,2,1,0:T(8,128)S(1)}, u32[]{:S(2)}, u32[]{:S(2)}) collective-permute-start(f32[1,2,128,128]{3,2,1,0:T(8,128)S(1)} %fusion.108), channel_id=1, source_target_pairs={{8,0},{16,8},{24,16},{32,24},{40,32},{48,40},{56,48},{64,56},{72,6... | collective-permute-start | bytes 393224 | tf_op jit(solution)/shard_map/while/body/eval_jaxpr/ppermute | solution.py:16
  169.8 9.0 %collective-permute-start.1 = (f32[1,2,128,128]{3,2,1,0:T(8,128)S(1)}, f32[1,2,128,128]{3,2,1,0:T(8,128)S(1)}, u32[]{:S(2)}, u32[]{:S(2)}) collective-permute-start(f32[1,2,128,128]{3,2,1,0:T(8,128)S(1)} %fusion.108), channel_id=1, source_target_pairs={{8,0},{16,8},{24,16},{32,24},{40,32},{48,40},{56,48},{64,56},{72,6... | collective-permute-start | bytes 393224 | tf_op jit(solution)/shard_map/while/body/eval_jaxpr/ppermute | solution.py:16
  182.1 9.2 %collective-permute-start.1 = (f32[1,2,128,128]{3,2,1,0:T(8,128)S(1)}, f32[1,2,128,128]{3,2,1,0:T(8,128)S(1)}, u32[]{:S(2)}, u32[]{:S(2)}) collective-permute-start(f32[1,2,128,128]{3,2,1,0:T(8,128)S(1)} %fusion.108), channel_id=1, source_target_pairs={{8,0},{16,8},{24,16},{32,24},{40,32},{48,40},{56,48},{64,56},{72,6... | collective-permute-start | bytes 393224 | tf_op jit(solution)/shard_map/while/body/eval_jaxpr/ppermute | solution.py:16
  194.6 10.5 %collective-permute-start.1 = (f32[1,2,128,128]{3,2,1,0:T(8,128)S(1)}, f32[1,2,128,128]{3,2,1,0:T(8,128)S(1)}, u32[]{:S(2)}, u32[]{:S(2)}) collective-permute-start(f32[1,2,128,128]{3,2,1,0:T(8,128)S(1)} %fusion.108), channel_id=1, source_target_pairs={{8,0},{16,8},{24,16},{32,24},{40,32},{48,40},{56,48},{64,56},{72,6... | collective-permute-start | bytes 393224 | tf_op jit(solution)/shard_map/while/body/eval_jaxpr/ppermute | solution.py:16
  208.3 9.9 %collective-permute-start.1 = (f32[1,2,128,128]{3,2,1,0:T(8,128)S(1)}, f32[1,2,128,128]{3,2,1,0:T(8,128)S(1)}, u32[]{:S(2)}, u32[]{:S(2)}) collective-permute-start(f32[1,2,128,128]{3,2,1,0:T(8,128)S(1)} %fusion.108), channel_id=1, source_target_pairs={{8,0},{16,8},{24,16},{32,24},{40,32},{48,40},{56,48},{64,56},{72,6... | collective-permute-start | bytes 393224 | tf_op jit(solution)/shard_map/while/body/eval_jaxpr/ppermute | solution.py:16
  258.3 9.0 %collective-permute-start.1 = (f32[1,2,128,128]{3,2,1,0:T(8,128)S(1)}, f32[1,2,128,128]{3,2,1,0:T(8,128)S(1)}, u32[]{:S(2)}, u32[]{:S(2)}) collective-permute-start(f32[1,2,128,128]{3,2,1,0:T(8,128)S(1)} %fusion.108), channel_id=1, source_target_pairs={{8,0},{16,8},{24,16},{32,24},{40,32},{48,40},{56,48},{64,56},{72,6... | collective-permute-start | bytes 393224 | tf_op jit(solution)/shard_map/while/body/eval_jaxpr/ppermute | solution.py:16
  319.8 9.0 %collective-permute-start.1 = (f32[1,2,128,128]{3,2,1,0:T(8,128)S(1)}, f32[1,2,128,128]{3,2,1,0:T(8,128)S(1)}, u32[]{:S(2)}, u32[]{:S(2)}) collective-permute-start(f32[1,2,128,128]{3,2,1,0:T(8,128)S(1)} %fusion.108), channel_id=1, source_target_pairs={{8,0},{16,8},{24,16},{32,24},{40,32},{48,40},{56,48},{64,56},{72,6... | collective-permute-start | bytes 393224 | tf_op jit(solution)/shard_map/while/body/eval_jaxpr/ppermute | solution.py:16
  332.1 9.1 %collective-permute-start.1 = (f32[1,2,128,128]{3,2,1,0:T(8,128)S(1)}, f32[1,2,128,128]{3,2,1,0:T(8,128)S(1)}, u32[]{:S(2)}, u32[]{:S(2)}) collective-permute-start(f32[1,2,128,128]{3,2,1,0:T(8,128)S(1)} %fusion.108), channel_id=1, source_target_pairs={{8,0},{16,8},{24,16},{32,24},{40,32},{48,40},{56,48},{64,56},{72,6... | collective-permute-start | bytes 393224 | tf_op jit(solution)/shard_map/while/body/eval_jaxpr/ppermute | solution.py:16
  344.4 10.2 %collective-permute-start.1 = (f32[1,2,128,128]{3,2,1,0:T(8,128)S(1)}, f32[1,2,128,128]{3,2,1,0:T(8,128)S(1)}, u32[]{:S(2)}, u32[]{:S(2)}) collective-permute-start(f32[1,2,128,128]{3,2,1,0:T(8,128)S(1)} %fusion.108), channel_id=1, source_target_pairs={{8,0},{16,8},{24,16},{32,24},{40,32},{48,40},{56,48},{64,56},{72,6... | collective-permute-start | bytes 393224 | tf_op jit(solution)/shard_map/while/body/eval_jaxpr/ppermute | solution.py:16
  357.9 9.9 %collective-permute-start.1 = (f32[1,2,128,128]{3,2,1,0:T(8,128)S(1)}, f32[1,2,128,128]{3,2,1,0:T(8,128)S(1)}, u32[]{:S(2)}, u32[]{:S(2)}) collective-permute-start(f32[1,2,128,128]{3,2,1,0:T(8,128)S(1)} %fusion.108), channel_id=1, source_target_pairs={{8,0},{16,8},{24,16},{32,24},{40,32},{48,40},{56,48},{64,56},{72,6... | collective-permute-start | bytes 393224 | tf_op jit(solution)/shard_map/while/body/eval_jaxpr/ppermute | solution.py:16
  371.0 9.0 %collective-permute-start.1 = (f32[1,2,128,128]{3,2,1,0:T(8,128)S(1)}, f32[1,2,128,128]{3,2,1,0:T(8,128)S(1)}, u32[]{:S(2)}, u32[]{:S(2)}) collective-permute-start(f32[1,2,128,128]{3,2,1,0:T(8,128)S(1)} %fusion.108), channel_id=1, source_target_pairs={{8,0},{16,8},{24,16},{32,24},{40,32},{48,40},{56,48},{64,56},{72,6... | collective-permute-start | bytes 393224 | tf_op jit(solution)/shard_map/while/body/eval_jaxpr/ppermute | solution.py:16
  383.3 9.0 %collective-permute-start.1 = (f32[1,2,128,128]{3,2,1,0:T(8,128)S(1)}, f32[1,2,128,128]{3,2,1,0:T(8,128)S(1)}, u32[]{:S(2)}, u32[]{:S(2)}) collective-permute-start(f32[1,2,128,128]{3,2,1,0:T(8,128)S(1)} %fusion.108), channel_id=1, source_target_pairs={{8,0},{16,8},{24,16},{32,24},{40,32},{48,40},{56,48},{64,56},{72,6... | collective-permute-start | bytes 393224 | tf_op jit(solution)/shard_map/while/body/eval_jaxpr/ppermute | solution.py:16
  395.6 9.0 %collective-permute-start.1 = (f32[1,2,128,128]{3,2,1,0:T(8,128)S(1)}, f32[1,2,128,128]{3,2,1,0:T(8,128)S(1)}, u32[]{:S(2)}, u32[]{:S(2)}) collective-permute-start(f32[1,2,128,128]{3,2,1,0:T(8,128)S(1)} %fusion.108), channel_id=1, source_target_pairs={{8,0},{16,8},{24,16},{32,24},{40,32},{48,40},{56,48},{64,56},{72,6... | collective-permute-start | bytes 393224 | tf_op jit(solution)/shard_map/while/body/eval_jaxpr/ppermute | solution.py:16
  511.6 13.7 %collective-permute-start.4 = (f32[1,128,16,128]{3,1,2,0:T(8,128)S(1)}, f32[1,128,16,128]{3,1,2,0:T(8,128)S(1)}, u32[]{:S(2)}, u32[]{:S(2)}) collective-permute-start(f32[1,128,16,128]{3,1,2,0:T(8,128)S(1)} %get-tuple-element.63), channel_id=1, source_target_pairs={{0,1},{1,2},{2,3},{3,4},{4,5},{5,6},{6,7},{8,9},{9,10},{10,11},{11... | collective-permute-start | bytes 3145736 | tf_op jit(solution)/shard_map/ppermute | solution.py:16
  513.5 16.1 %collective-permute-start.5 = (f32[1,128,16,128]{3,1,2,0:T(8,128)S(1)}, f32[1,128,16,128]{3,1,2,0:T(8,128)S(1)}, u32[]{:S(2)}, u32[]{:S(2)}) collective-permute-start(f32[1,128,16,128]{3,1,2,0:T(8,128)S(1)} %get-tuple-element.62), channel_id=1, source_target_pairs={{1,0},{2,1},{3,2},{4,3},{5,4},{6,5},{7,6},{9,8},{10,9},{11,10},{12... | collective-permute-start | bytes 3145736 | tf_op jit(solution)/shard_map/ppermute | solution.py:16
  597.3 13.7 %collective-permute-start.6 = (f32[1,128,16,128]{3,1,2,0:T(8,128)S(1)}, f32[1,128,16,128]{3,1,2,0:T(8,128)S(1)}, u32[]{:S(2)}, u32[]{:S(2)}) collective-permute-start(f32[1,128,16,128]{3,1,2,0:T(8,128)S(1)} %get-tuple-element.59), channel_id=1, source_target_pairs={{0,1},{1,2},{2,3},{3,4},{4,5},{5,6},{6,7},{8,9},{9,10},{10,11},{11... | collective-permute-start | bytes 3145736 | tf_op jit(solution)/shard_map/ppermute | solution.py:16
  599.3 16.1 %collective-permute-start.7 = (f32[1,128,16,128]{3,1,2,0:T(8,128)S(1)}, f32[1,128,16,128]{3,1,2,0:T(8,128)S(1)}, u32[]{:S(2)}, u32[]{:S(2)}) collective-permute-start(f32[1,128,16,128]{3,1,2,0:T(8,128)S(1)} %get-tuple-element.58), channel_id=1, source_target_pairs={{1,0},{2,1},{3,2},{4,3},{5,4},{6,5},{7,6},{9,8},{10,9},{11,10},{12... | collective-permute-start | bytes 3145736 | tf_op jit(solution)/shard_map/ppermute | solution.py:16
  (56 other events, 391.1 us)
where the time goes:
time: 667 us; the launch traced here: 661 us
  waiting for transfers between devices  197 us (30%)
  starting transfers between devices  181 us (27%)
  blocking collectives  138 us (21%)
  matrix products  87.7 us (13%)
  other arithmetic  34.1 us (5%)
  between operations  14.2 us (2%)
  local copies, waits for them, and re-layouts  7.36 us (1%)
    ppermute x68, waiting for transfers between devices, shifted(): return lax.ppermute(block, axis, route)  197 us
    ppermute x68, starting transfers between devices, shifted(): return lax.ppermute(block, axis, route)  181 us
    psum x2, blocking collectives, per_device(): correlation = lax.psum(jnp.sum(wave * applied), 'sector')  62.5 us
    psum x2, blocking collectives, per_device(): res_norm = lax.psum(jnp.sum(residual * residual), 'sector')  26.2 us
    psum x2, blocking collectives, per_device(): lax.psum((jnp.sum(unit_dir * turned), jnp.sum(applied * unit_dir)), 'sect...  20.2 us
    dot_general x62, matrix products, advance(): jnp.einsum('...ji,...jl,...lm->...im', transfer, left_now, transfer, prec...  20.2 us
    dot_general x62, matrix products, advance(): jnp.einsum('...ij,...jl,...ml->...im', transfer, right_now, transfer, pre...  20.1 us
    dot_general x3, matrix products, apply_products(): lowered = jnp.einsum('kba,kbpc->kapc', coupler, above, precision=HIGHEST)  16.1 us
  transfers between devices with their start and end apart: 68, of which 41 were waited for; matrix products, arithmetic and copies ran while one was open for 10% of the time, Pallas kernels for 0%

commit v1 on v0

--- a/solution.py
+++ b/solution.py
@@ -1,13 +1,230 @@
+import functools
+
 import jax
 import jax.numpy as jnp
 from jax import lax
+from jax.experimental import pallas as pl
+from jax.experimental.pallas import tpu as pltpu
 from jax.sharding import PartitionSpec as P
 
 ITERS = 2
-
+BLK = 128
+NX = 4
+NZ = 8
 
 HIGHEST = lax.Precision.HIGHEST
 EPS = 1e-06
+MESH = pl.DeviceIdType.MESH
+F32 = jnp.float32
+NN = (((1,), (0,)), ((), ()))
+NT = (((1,), (1,)), ((), ()))
+
+
+def halves(value):
+    high = value.astype(jnp.bfloat16)
+    return high, (value - high.astype(F32)).astype(jnp.bfloat16)
+
+
+def dot(lhs, rhs, dims):
+    return lax.dot_general(lhs, rhs, dims, preferred_element_type=F32)
+
+
+def product(lhs, rhs, dims=NN):
+    lhs_high, lhs_low = halves(lhs)
+    rhs_high, rhs_low = halves(rhs)
+    both = jnp.concatenate([lhs_high, lhs_low], axis=1)
+    twice = jnp.concatenate([rhs_high, rhs_high], axis=1 if dims is NT else 0)
+    return dot(both, twice, dims) + dot(lhs_high, rhs_low, dims)
+
+
+def carry_over(matrix, env, source):
+    return product(product(matrix, env), matrix, NT) + source
+
+
+def env_kernel(t_ref, e_ref, left_ref, right_ref, mine, elements, window, came, far, ends, envs,
+               send_a, recv_a, send_z, recv_z, send_e, recv_e):
+    chain = lax.axis_index("chain")
+    sector = lax.axis_index("sector")
+    x = lax.rem(chain, NX)
+    z = lax.div(chain, NX)
+    odd = lax.rem(x, 2)
+    zz = z + odd * (NZ - 1 - 2 * z)
+    my_slot = x + odd * (NX - 1 - 2 * x)
+
+    def in_row(other):
+        return (z * NX + other, sector)
+
+    def in_column(other):
+        return ((other + odd * (NZ - 1 - 2 * other)) * NX + x, sector)
+
+    def slot_of(column):
+        return x if column % 2 == 0 else NX - 1 - x
+
+    for k in range(2):
+        transfer = t_ref[k]
+        source = 0.5 * (e_ref[k] + e_ref[k].T)
+        mine[2 * k, :BLK] = transfer.T
+        mine[2 * k + 1, :BLK] = transfer
+        mine[2 * k, BLK:] = source
+        mine[2 * k + 1, BLK:] = source
+    came[...] = jnp.zeros_like(came)
+    far[...] = jnp.zeros_like(far)
+
+    barrier = pltpu.get_barrier_semaphore()
+    greeted = 0
+    for hop in range(1, NX):
+        pl.semaphore_signal(barrier, inc=1, device_id=in_row(lax.rem(x + hop, NX)), device_id_type=MESH)
+        greeted = greeted + 1
+    for hop in (1, 2, 5):
+        for other, there in ((zz + hop, zz + hop < NZ), (zz - hop, zz >= hop)):
+            @pl.when(there)
+            def _():
+                pl.semaphore_signal(barrier, inc=1, device_id=in_column(other), device_id_type=MESH)
+            greeted = greeted + there.astype(jnp.int32)
+    pl.semaphore_wait(barrier, greeted)
+
+    def deal(column):
+        slot = slot_of(column)
+        return pltpu.make_async_remote_copy(
+            mine.at[column], elements.at[slot], send_a.at[column], recv_a.at[slot],
+            device_id=in_row(column), device_id_type=MESH)
+
+    for column in range(NX):
+        @pl.when(x != column)
+        def _():
+            deal(column).start()
+    elements[pl.ds(my_slot, 1)] = mine[pl.ds(x, 1)]
+    for slot in range(NX):
+        @pl.when(my_slot != slot)
+        def _():
+            pltpu.make_async_remote_copy(
+                mine.at[slot], elements.at[slot], send_a.at[slot], recv_a.at[slot],
+                device_id=in_row(lax.rem(x + 1, NX)), device_id_type=MESH).wait_recv()
+
+    q0, q1, q2, q3 = [elements[s, :BLK] for s in range(NX)]
+    s0, s1, s2, s3 = [elements[s, BLK:] for s in range(NX)]
+    q01 = product(q1, q0)
+    y01 = carry_over(q1, s0, s1)
+    q23 = product(q3, q2)
+    y23 = carry_over(q3, s2, s3)
+    qw = product(q23, q01)
+    yw = carry_over(q23, y01, y23)
+
+    def step(at, hop):
+        return pltpu.make_async_remote_copy(
+            window.at[at], came.at[at], send_z.at[at], recv_z.at[at],
+            device_id=in_column(zz + hop), device_id_type=MESH)
+
+    def receive(at, hop):
+        @pl.when(zz >= hop)
+        def _():
+            pltpu.make_async_remote_copy(
+                window.at[at], came.at[at], send_z.at[at], recv_z.at[at],
+                device_id=in_column(zz - hop), device_id_type=MESH).wait_recv()
+
+    for at, hop in ((0, 1), (1, 2)):
+        window[at, :BLK] = qw
+        window[at, BLK:] = yw
+        @pl.when(zz + hop < NZ)
+        def _():
+            step(at, hop).start()
+        if at == 0:
+            q012 = product(q2, q01)
+            y012 = carry_over(q2, y01, s2)
+        receive(at, hop)
+        qp, yp = came[at, :BLK], came[at, BLK:]
+        qn = product(qw, qp)
+        yw = carry_over(qw, yp, yw)
+        qw = qn
+
+    window[2, :BLK] = qw
+    window[2, BLK:] = yw
+    far_copy = pltpu.make_async_remote_copy(
+        window.at[2, pl.ds(BLK, BLK)], far, send_z.at[3], recv_z.at[3],
+        device_id=in_column(zz + 5), device_id_type=MESH)
+
+    @pl.when(zz + 1 < NZ)
+    def _():
+        step(2, 1).start()
+
+    @pl.when(zz + 5 < NZ)
+    def _():
+        far_copy.start()
+
+    @pl.when(zz >= 5)
+    def _():
+        pltpu.make_async_remote_copy(
+            window.at[2, pl.ds(BLK, BLK)], far, send_z.at[3], recv_z.at[3],
+            device_id=in_column(zz - 5), device_id_type=MESH).wait_recv()
+    receive(2, 1)
+    start = carry_over(came[2, :BLK], far[...], came[2, BLK:])
+
+    def owner(slot):
+        return slot + odd * (NX - 1 - 2 * slot)
+
+    def give(slot):
+        return pltpu.make_async_remote_copy(
+            ends.at[slot], envs.at[x], send_e.at[slot], recv_e.at[x],
+            device_id=in_row(owner(slot)), device_id_type=MESH)
+
+    for slot, (q, y) in enumerate(((None, None), (q0, s0), (q01, y01), (q012, y012))):
+        ends[slot] = start if slot == 0 else carry_over(q, start, y)
+        @pl.when(my_slot != slot)
+        def _():
+            give(slot).start()
+    envs[pl.ds(x, 1)] = ends[pl.ds(my_slot, 1)]
+    for column in range(NX):
+        @pl.when(x != column)
+        def _():
+            pltpu.make_async_remote_copy(
+                ends.at[column], envs.at[column], send_e.at[column], recv_e.at[column],
+                device_id=in_row(column), device_id_type=MESH).wait_recv()
+    for k in range(2):
+        left_ref[k] = envs[2 * k]
+        right_ref[k] = envs[2 * k + 1]
+
+    for column in range(NX):
+        @pl.when(x != column)
+        def _():
+            deal(column).wait_send()
+    for at, hop in ((0, 1), (1, 2), (2, 1)):
+        @pl.when(zz + hop < NZ)
+        def _():
+            step(at, hop).wait_send()
+    @pl.when(zz + 5 < NZ)
+    def _():
+        far_copy.wait_send()
+    for slot in range(NX):
+        @pl.when(my_slot != slot)
+        def _():
+            give(slot).wait_send()
+
+
+def environments(transfer, energy_terms):
+    pair = jax.ShapeDtypeStruct((2, BLK, BLK), F32)
+    vmem = pl.BlockSpec(memory_space=pltpu.VMEM)
+    return pl.pallas_call(
+        env_kernel,
+        out_shape=(pair, pair),
+        in_specs=[vmem, vmem],
+        out_specs=(vmem, vmem),
+        scratch_shapes=[
+            pltpu.VMEM((NX, 2 * BLK, BLK), F32),
+            pltpu.VMEM((NX, 2 * BLK, BLK), F32),
+            pltpu.VMEM((3, 2 * BLK, BLK), F32),
+            pltpu.VMEM((3, 2 * BLK, BLK), F32),
+            pltpu.VMEM((BLK, BLK), F32),
+            pltpu.VMEM((NX, BLK, BLK), F32),
+            pltpu.VMEM((NX, BLK, BLK), F32),
+            pltpu.SemaphoreType.DMA((NX,)),
+            pltpu.SemaphoreType.DMA((NX,)),
+            pltpu.SemaphoreType.DMA((4,)),
+            pltpu.SemaphoreType.DMA((4,)),
+            pltpu.SemaphoreType.DMA((NX,)),
+            pltpu.SemaphoreType.DMA((NX,)),
+        ],
+        compiler_params=pltpu.CompilerParams(collective_id=0, has_side_effects=True),
+    )(transfer, energy_terms)
 
 
 def shifted(block, axis, distance):
@@ -38,28 +255,8 @@
 
 
 def per_device(wave_start, transfer, energy_terms, coupling, physical, kept_ranks):
-    sources = symmetric(energy_terms)
-    zero_env = jnp.zeros_like(transfer)
-
-    def advance(turn_index, carry):
-        left_now, right_now = carry
-        left_out = (
-            jnp.einsum("...ji,...jl,...lm->...im", transfer, left_now, transfer, precision=HIGHEST)
-            + sources
-        )
-        right_out = (
-            jnp.einsum("...ij,...jl,...ml->...im", transfer, right_now, transfer, precision=HIGHEST)
-            + sources
-        )
-        left_next = shifted(left_out, "chain", 1)
-        right_next = shifted(right_out, "chain", -1)
-        return (left_next, right_next)
-
-    left_env, right_env = lax.fori_loop(
-        0, lax.axis_size("chain") - 1, advance, (zero_env, zero_env)
-    )
-    left_blk = left_env[0]
-    right_blk = right_env[0]
+    left_blk, right_blk = environments(transfer[0], energy_terms[0])
+    left_env = left_blk[None]
     sym_phys = symmetric(physical[0])
     coupler = coupling[0]
 

time: 667 us -> 279 us (0.42)
  the two profiles are of different devices: /device:TPU:103 before, /device:TPU:1 now
where the time goes in v1:
time: 279 us; the launch traced here: 275 us
  blocking collectives  111 us (40%)
  matrix products  44.5 us (16%)
  Pallas kernels  36 us (13%)
  other arithmetic  34.1 us (12%)
  starting transfers between devices  14.4 us (5%)
  between operations  14.2 us (5%)
  waiting for transfers between devices  13.3 us (5%)
  local copies, waits for them, and re-layouts  6.7 us (2%)
    pallas_call x1, Pallas kernels, environments(): pl.pallas_call(env_kernel, out_shape=(pair, pair), in_specs=[vmem, vmem],...  36 us
    psum x2, blocking collectives, per_device(): correlation = lax.psum(jnp.sum(wave * applied), 'sector')  33.4 us
    psum x2, blocking collectives, per_device(): res_norm = lax.psum(jnp.sum(residual * residual), 'sector')  26.3 us
    psum x2, blocking collectives, per_device(): lax.psum((jnp.sum(unit_dir * turned), jnp.sum(applied * unit_dir)), 'sect...  20.2 us
    dot_general x3, matrix products, apply_products(): lowered = jnp.einsum('kba,kbpc->kapc', coupler, above, precision=HIGHEST)  16.1 us
    psum x1, blocking collectives, per_device(): kept_total = lax.psum(jnp.sum(truncated * truncated), 'sector')  15.9 us
    psum x1, blocking collectives, per_device(): norm_start = lax.psum(jnp.sum(wave * wave), 'sector')  15.6 us
    ppermute x6, starting transfers between devices, shifted(): return lax.ppermute(block, axis, route)  14.4 us
  transfers between devices with their start and end apart: 6, of which 4 were waited for; matrix products, arithmetic and copies ran while one was open for 9% of the time, Pallas kernels for 13%

profile of v1, /device:TPU:1, one launch (start us, length us, event | category | flops | bytes accessed | tf_op | source)
XLA Modules:
  0.0 274.5 jit_solution(15818804410242326289)
XLA Ops:
  3.5 15.6 %psum.70 = f32[]{:T(128)} all-reduce(f32[]{:T(128)} %multiply_reduce_fusion.8), channel_id=1, replica_groups=mesh['chain'=32,'sector'=8] {'sector'}, use_global_device_ids=true, to_apply=%region_1.0 | all-reduce | flops 1 | bytes 8 | tf_op jit(solution)/shard_map/psum | solution.py:267
  27.1 3.7 %collective-permute-start.1 = (f32[1,128,16,128]{3,1,2,0:T(8,128)}, f32[1,128,16,128]{3,1,2,0:T(8,128)}, u32[]{:S(2)}, u32[]{:S(2)}) collective-permute-start(f32[1,128,16,128]{3,1,2,0:T(8,128)} %get-tuple-element.30), channel_id=1, source_target_pairs={{1,0},{2,1},{3,2},{4,3},{5,4},{6,5},{7,6},{9,8},{10,9},{11,10},{12... | collective-permute-start | bytes 3145736 | tf_op jit(solution)/shard_map/ppermute | solution.py:233
  32.9 36.0 %shard_map.85 = (f32[2,128,128]{2,1,0:T(8,128)}, f32[2,128,128]{2,1,0:T(8,128)}) custom-call(f32[2,128,128]{2,1,0:T(8,128)} %bitcast.127, f32[2,128,128]{2,1,0:T(8,128)} %bitcast.128), custom_call_target="tpu_custom_call" | custom-call | tf_op jit(solution)/shard_map/pallas_call | solution.py:206
  68.9 4.7 %fusion.21 = f32[2,128,128,16]{2,3,1,0:T(8,128)S(1)} fusion(f32[2,128,16,128]{3,1,2,0:T(8,128)} %fusion.71, f32[16,16]{0,1:T(8,128)S(1)} %copy.10, f32[1,16,16]{2,1,0:T(8,128)S(1)} %copy-done.8), kind=kOutput, calls=%fused_computation.27 | convolution fusion | flops 100663808 | bytes 4196352 | tf_op jit(solution)/shard_map/pq,kaqc->kapc/dot_general | solution.py:243
  77.6 6.7 %multiply_reduce_fusion.7 = (f32[]{:T(128)}, f32[2,128,16,128]{3,1,2,0:T(8,128)}) fusion(f32[1,2,128,16,128]{4,2,3,1,0:T(8,128)S(1)} %copy-done.3, f32[1,2,128,128]{3,2,1,0:T(8,128)S(1)} %copy-done, f32[1,128,16,128]{3,1,2,0:T(8,128)} %collective-permute-done.1, f32[1,128,16,128]{3,1,2,0:T(8,128)S(1)} %copy-done.5, ...), kind=kOutput, calls=%fused_computation.43 | convolution fusion | flops 809500672 | bytes 14811140 | tf_op jit(solution)/shard_map/kba,kbpc->kapc/dot_general | solution.py:253
  84.3 17.5 %psum.71 = f32[]{:T(128)} all-reduce(f32[]{:T(128)} %get-tuple-element.33), channel_id=1, replica_groups=mesh['chain'=32,'sector'=8] {'sector'}, use_global_device_ids=true, to_apply=%region_3.0 | all-reduce | flops 1 | bytes 8 | tf_op jit(solution)/shard_map/psum | solution.py:272
  101.8 3.6 %multiply_reduce_fusion.6 = f32[]{:T(128)} fusion(f32[2,128,16,128]{3,1,2,0:T(8,128)} %get-tuple-element.34, f32[]{:T(128)} %psum.71, f32[]{:T(128)S(6)} %sqrt.24, f32[1,2,128,16,128]{4,3,2,1,0:T(8,128)S(1)} %copy-done.1), kind=kLoop, calls=%fused_computation.41 | loop fusion | flops 2621439 | bytes 4194316 | tf_op jit(solution)/shard_map/reduce_sum | solution.py:274
  105.3 13.0 %psum.72 = f32[]{:T(128)} all-reduce(f32[]{:T(128)} %multiply_reduce_fusion.6), channel_id=1, replica_groups=mesh['chain'=32,'sector'=8] {'sector'}, use_global_device_ids=true, to_apply=%region_5.0 | all-reduce | flops 1 | bytes 8 | tf_op jit(solution)/shard_map/psum | solution.py:274
  119.1 3.6 %broadcast_divide_fusion.1 = f32[2,128,16,128]{3,1,2,0:T(8,128)S(1)} fusion(f32[]{:T(128)S(6)} %sqrt.25, f32[2,128,16,128]{3,1,2,0:T(8,128)} %get-tuple-element.34, f32[]{:T(128)} %psum.71, f32[]{:T(128)S(6)} %sqrt.24, f32[1,2,128,16,128]{4,3,2,1,0:T(8,128)} %param.6), kind=kLoop, calls=%fused_computation.51 | loop fusion | flops 2097152 | bytes 6291468 | tf_op jit(solution)/shard_map/div | solution.py:275
  129.4 3.1 %fusion.19 = f32[2,128,128,16]{2,3,1,0:T(8,128)S(1)} fusion(f32[2,128,16,128]{3,1,2,0:T(8,128)S(1)} %broadcast_divide_fusion.1, f32[16,16]{0,1:T(8,128)S(1)} %copy.10, f32[1,16,16]{2,1,0:T(8,128)S(1)} %copy-done.8), kind=kOutput, calls=%fused_computation.25 | convolution fusion | flops 100663808 | bytes 4196352 | tf_op jit(solution)/shard_map/pq,kaqc->kapc/dot_general | solution.py:243
  138.7 4.4 %collective-permute-done.3 = f32[1,128,16,128]{3,1,2,0:T(8,128)S(1)} collective-permute-done((f32[1,128,16,128]{3,1,2,0:T(8,128)S(1)}, f32[1,128,16,128]{3,1,2,0:T(8,128)S(1)}, u32[]{:S(2)}, u32[]{:S(2)}) %collective-permute-start.3) | collective-permute-done | bytes 1048608 | tf_op jit(solution)/shard_map/ppermute | solution.py:233
  143.1 5.6 %multiply_reduce_fusion.4 = (f32[]{:T(128)}, f32[]{:T(128)}, f32[2,128,16,128]{3,1,2,0:T(8,128)}) fusion(f32[2,128,16,128]{3,1,2,0:T(8,128)S(1)} %broadcast_divide_fusion.1, f32[2,128,16,128]{3,1,2,0:T(8,128)S(1)} %copy-done.4, f32[1,2,128,128]{3,2,1,0:T(8,128)S(1)} %copy-done, f32[1,128,16,128]{3,1,2,0:T(8,128)S(1)} %collective-permute-done.3, ...), kind=kOutput, calls=%fused_computation.39 | convolution fusion | flops 810549248 | bytes 16908296 | tf_op jit(solution)/shard_map/kba,kbpc->kapc/dot_general | solution.py:253
  148.7 10.1 %all-reduce.1 = (f32[]{:T(128)}, f32[]{:T(128)}) all-reduce(f32[]{:T(128)} %get-tuple-element.11, f32[]{:T(128)} %get-tuple-element.10), channel_id=1, replica_groups=mesh['chain'=32,'sector'=8] {'sector'}, use_global_device_ids=true, to_apply=%region_7.0 | all-reduce | flops 2 | bytes 16 | tf_op jit(solution)/shard_map/psum | solution.py:277
  163.3 7.2 %multiply_reduce_fusion.3 = (f32[]{:T(128)}, f32[2,128,16,128]{3,1,2,0:T(8,128)}, f32[2,128,16,128]{3,1,2,0:T(8,128)}) fusion(f32[]{:T(128)S(6)} %sqrt.27, f32[2,128,16,128]{3,1,2,0:T(8,128)S(1)} %broadcast_divide_fusion.1, f32[]{:T(128)S(6)} %sub.27, f32[]{:T(128)} %get-tuple-element.14, f32[2,128,16,128]{3,1,2,0:T(8,128)} %get-tuple-element.35, ...), kind=kLoop, calls=%fused_computation.36 | loop fusion | flops 5767167 | bytes 12582932 | tf_op jit(solution)/shard_map/reduce_sum | solution.py:272
  170.5 15.9 %psum.75 = f32[]{:T(128)} all-reduce(f32[]{:T(128)} %get-tuple-element.18), channel_id=1, replica_groups=mesh['chain'=32,'sector'=8] {'sector'}, use_global_device_ids=true, to_apply=%region_11.0 | all-reduce | flops 1 | bytes 8 | tf_op jit(solution)/shard_map/psum | solution.py:272
  186.3 4.0 %multiply_reduce_fusion.2 = f32[]{:T(128)} fusion(f32[2,128,16,128]{3,1,2,0:T(8,128)} %get-tuple-element.20, f32[2,128,16,128]{3,1,2,0:T(8,128)} %get-tuple-element.19, f32[]{:T(128)} %psum.75), kind=kLoop, calls=%fused_computation.34 | loop fusion | flops 2097151 | bytes 4194312 | tf_op jit(solution)/shard_map/reduce_sum | solution.py:274
  190.4 13.2 %psum.76 = f32[]{:T(128)} all-reduce(f32[]{:T(128)} %multiply_reduce_fusion.2), channel_id=1, replica_groups=mesh['chain'=32,'sector'=8] {'sector'}, use_global_device_ids=true, to_apply=%region_13.0 | all-reduce | flops 1 | bytes 8 | tf_op jit(solution)/shard_map/psum | solution.py:274
  204.3 4.1 %multiply_reduce_fusion.1 = (f32[]{:T(128)}, f32[2,128,16,128]{3,1,2,0:T(8,128)S(1)}) fusion(f32[2,128,16,128]{3,1,2,0:T(8,128)} %get-tuple-element.20, f32[]{:T(128)S(6)} %sqrt.28, f32[2,128,16,128]{3,1,2,0:T(8,128)} %get-tuple-element.19, f32[]{:T(128)} %psum.75), kind=kLoop, calls=%fused_computation.33 | loop fusion | flops 2621439 | bytes 6291468 | tf_op jit(solution)/shard_map/reduce_sum | solution.py:278
  215.2 3.1 %fusion.17 = f32[2,128,128,16]{2,3,1,0:T(8,128)S(1)} fusion(f32[2,128,16,128]{3,1,2,0:T(8,128)S(1)} %get-tuple-element.17, f32[16,16]{0,1:T(8,128)S(1)} %copy.10, f32[1,16,16]{2,1,0:T(8,128)S(1)} %copy-done.8), kind=kOutput, calls=%fused_computation.23 | convolution fusion | flops 100663808 | bytes 4196352 | tf_op jit(solution)/shard_map/pq,kaqc->kapc/dot_general | solution.py:243
  224.4 4.4 %collective-permute-done.5 = f32[1,128,16,128]{3,1,2,0:T(8,128)S(1)} collective-permute-done((f32[1,128,16,128]{3,1,2,0:T(8,128)S(1)}, f32[1,128,16,128]{3,1,2,0:T(8,128)S(1)}, u32[]{:S(2)}, u32[]{:S(2)}) %collective-permute-start.5) | collective-permute-done | bytes 1048608 | tf_op jit(solution)/shard_map/ppermute | solution.py:233
  228.8 3.8 %fusion.12 = f32[]{:T(128)} fusion(f32[2,128,16,128]{3,1,2,0:T(8,128)S(1)} %get-tuple-element.17, f32[1,128,16,128]{3,1,2,0:T(8,128)S(1)} %get-tuple-element.24, f32[1,128,16,128]{3,1,2,0:T(8,128)S(1)} %collective-permute-done.4, f32[2,128,128,16]{2,3,1,0:T(8,128)S(1)} %fusion.17, f32[2,128,16,128]{3,1,2,0:T(8,128)S(1)} %fusion.35, ...), kind=kOutput, calls=%fused_computation.15 | convolution fusion | flops 809500672 | bytes 12713988 | tf_op jit(solution)/shard_map/kba,kbpc->kapc/dot_general | solution.py:253
  232.6 10.2 %all-reduce = (f32[]{:T(128)}, f32[]{:T(128)}) all-reduce(f32[]{:T(128)} %get-tuple-element.16, f32[]{:T(128)} %fusion.12), channel_id=1, replica_groups=mesh['chain'=32,'sector'=8] {'sector'}, use_global_device_ids=true, to_apply=%region_15.0 | all-reduce | flops 2 | bytes 16 | tf_op jit(solution)/shard_map/psum | solution.py:277
  247.3 3.4 %multiply_reduce_fusion = f32[]{:T(128)} fusion(f32[2,128]{1,0:T(2,128)S(1)} %compare_convert_fusion, f32[]{:T(128)S(6)} %sqrt.30, f32[2,128,16,128]{3,1,2,0:T(8,128)S(1)} %get-tuple-element.17, f32[]{:T(128)S(6)} %sub.31, f32[2,128,16,128]{3,1,2,0:T(8,128)} %get-tuple-element.19, f32[]{:T(128)} %get-tuple-element.12), kind=kLoop, calls=%fused_computation.31 | loop fusion | flops 3670015 | bytes 4195344 | tf_op jit(solution)/shard_map/reduce_sum | solution.py:290
  250.7 15.9 %psum.79 = f32[]{:T(128)} all-reduce(f32[]{:T(128)} %multiply_reduce_fusion), channel_id=1, replica_groups=mesh['chain'=32,'sector'=8] {'sector'}, use_global_device_ids=true, to_apply=%region_19.0 | all-reduce | flops 1 | bytes 8 | tf_op jit(solution)/shard_map/psum | solution.py:290
  (52 shorter events, 47.7 us)
Async XLA Ops:
  0.6 19.9 %copy-start = (f32[1,2,128,128]{3,2,1,0:T(8,128)S(1)}, f32[1,2,128,128]{3,2,1,0:T(8,128)}, u32[]{:S(2)}) copy-start(f32[1,2,128,128]{3,2,1,0:T(8,128)} %param.9) | copy-start | bytes 393220
  0.6 19.2 %copy-start.1 = (f32[1,2,128,16,128]{4,3,2,1,0:T(8,128)S(1)}, f32[1,2,128,16,128]{4,3,2,1,0:T(8,128)}, u32[]{:S(2)}) copy-start(f32[1,2,128,16,128]{4,3,2,1,0:T(8,128)} %param.6) | copy-start | bytes 6291460
  20.5 5.1 %copy-start.2 = (f32[1,2,128,16,128]{4,2,3,1,0:T(8,128)}, f32[1,2,128,16,128]{4,2,3,1,0:T(8,128)S(1)}, u32[]{:S(2)}) copy-start(f32[1,2,128,16,128]{4,2,3,1,0:T(8,128)S(1)} %copy_divide_fusion) | copy-start | bytes 6291460
  23.7 53.8 %collective-permute-start = (f32[1,128,16,128]{3,1,2,0:T(8,128)}, f32[1,128,16,128]{3,1,2,0:T(8,128)}, u32[]{:S(2)}, u32[]{:S(2)}) collective-permute-start(f32[1,128,16,128]{3,1,2,0:T(8,128)} %get-tuple-element.31), channel_id=1, source_target_pairs={{0,1},{1,2},{2,3},{3,4},{4,5},{5,6},{6,7},{8,9},{9,10},{10,11},{11... | collective-permute-start | bytes 3145736 | tf_op jit(solution)/shard_map/ppermute | solution.py:233
  27.1 5.7 %copy-start.8 = (f32[1,16,16]{2,1,0:T(8,128)S(1)}, f32[1,16,16]{2,1,0:T(8,128)}, u32[]{:S(2)}) copy-start(f32[1,16,16]{2,1,0:T(8,128)} %param.10) | copy-start | bytes 3076
  27.1 50.4 %collective-permute-start.1 = (f32[1,128,16,128]{3,1,2,0:T(8,128)}, f32[1,128,16,128]{3,1,2,0:T(8,128)}, u32[]{:S(2)}, u32[]{:S(2)}) collective-permute-start(f32[1,128,16,128]{3,1,2,0:T(8,128)} %get-tuple-element.30), channel_id=1, source_target_pairs={{1,0},{2,1},{3,2},{4,3},{5,4},{6,5},{7,6},{9,8},{10,9},{11,10},{12... | collective-permute-start | bytes 3145736 | tf_op jit(solution)/shard_map/ppermute | solution.py:233
  68.9 4.7 %copy-start.3 = (f32[1,2,128,16,128]{4,2,3,1,0:T(8,128)S(1)}, f32[1,2,128,16,128]{4,2,3,1,0:T(8,128)}, u32[]{:S(2)}) copy-start(f32[1,2,128,16,128]{4,2,3,1,0:T(8,128)} %copy-done.2) | copy-start | bytes 6291460
  68.9 4.7 %copy-start.6 = (f32[2,128,128]{2,1,0:T(8,128)S(1)}, f32[2,128,128]{2,1,0:T(8,128)}, u32[]{:S(2)}) copy-start(f32[2,128,128]{2,1,0:T(8,128)} %get-tuple-element.5) | copy-start | bytes 393220
  73.6 2.0 copy-start.7
  75.6 2.0 copy-start.5
  125.0 13.7 %collective-permute-start.2 = (f32[1,128,16,128]{3,1,2,0:T(8,128)S(1)}, f32[1,128,16,128]{3,1,2,0:T(8,128)S(1)}, u32[]{:S(2)}, u32[]{:S(2)}) collective-permute-start(f32[1,128,16,128]{3,1,2,0:T(8,128)S(1)} %get-tuple-element.27), channel_id=1, source_target_pairs={{0,1},{1,2},{2,3},{3,4},{4,5},{5,6},{6,7},{8,9},{9,10},{10,11},{11... | collective-permute-start | bytes 3145736 | tf_op jit(solution)/shard_map/ppermute | solution.py:233
  127.0 16.1 %collective-permute-start.3 = (f32[1,128,16,128]{3,1,2,0:T(8,128)S(1)}, f32[1,128,16,128]{3,1,2,0:T(8,128)S(1)}, u32[]{:S(2)}, u32[]{:S(2)}) collective-permute-start(f32[1,128,16,128]{3,1,2,0:T(8,128)S(1)} %get-tuple-element.26), channel_id=1, source_target_pairs={{1,0},{2,1},{3,2},{4,3},{5,4},{6,5},{7,6},{9,8},{10,9},{11,10},{12... | collective-permute-start | bytes 3145736 | tf_op jit(solution)/shard_map/ppermute | solution.py:233
  134.5 8.6 %copy-start.4 = (f32[2,128,16,128]{3,1,2,0:T(8,128)S(1)}, f32[2,128,16,128]{3,1,2,0:T(8,128)}, u32[]{:S(2)}) copy-start(f32[2,128,16,128]{3,1,2,0:T(8,128)} %get-tuple-element.34) | copy-start | bytes 6291460
  210.5 4.6 %copy-start.9 = (s32[1,2]{1,0:T(1,128)S(1)}, s32[1,2]{1,0:T(1,128)}, u32[]{:S(2)}) copy-start(s32[1,2]{1,0:T(1,128)} %param.11) | copy-start | bytes 28
  210.8 13.7 %collective-permute-start.4 = (f32[1,128,16,128]{3,1,2,0:T(8,128)S(1)}, f32[1,128,16,128]{3,1,2,0:T(8,128)S(1)}, u32[]{:S(2)}, u32[]{:S(2)}) collective-permute-start(f32[1,128,16,128]{3,1,2,0:T(8,128)S(1)} %get-tuple-element.23), channel_id=1, source_target_pairs={{0,1},{1,2},{2,3},{3,4},{4,5},{5,6},{6,7},{8,9},{9,10},{10,11},{11... | collective-permute-start | bytes 3145736 | tf_op jit(solution)/shard_map/ppermute | solution.py:233
  212.7 16.1 %collective-permute-start.5 = (f32[1,128,16,128]{3,1,2,0:T(8,128)S(1)}, f32[1,128,16,128]{3,1,2,0:T(8,128)S(1)}, u32[]{:S(2)}, u32[]{:S(2)}) collective-permute-start(f32[1,128,16,128]{3,1,2,0:T(8,128)S(1)} %get-tuple-element.22), channel_id=1, source_target_pairs={{1,0},{2,1},{3,2},{4,3},{5,4},{6,5},{7,6},{9,8},{10,9},{11,10},{12... | collective-permute-start | bytes 3145736 | tf_op jit(solution)/shard_map/ppermute | solution.py:233

commit v2 on v1

v2 whole, which is shorter than its diff:
```python
import functools

import jax
import jax.numpy as jnp
from jax import lax
from jax.experimental import pallas as pl
from jax.experimental.pallas import tpu as pltpu
from jax.sharding import PartitionSpec as P

BLK = 128
PHYS = 16
NX = 4
NZ = 8
NS = 8
ROWS = BLK * PHYS
CHUNKS = 4
CHUNK = PHYS // CHUNKS
PAIRS = PHYS // 2

EPS = 1e-06
MESH = pl.DeviceIdType.MESH
F32 = jnp.float32
BF16 = jnp.bfloat16
NN = (((1,), (0,)), ((), ()))
NT = (((1,), (1,)), ((), ()))


def halves(value):
    high = value.astype(BF16)
    return high, (value - high.astype(F32)).astype(BF16)


def dot(lhs, rhs, dims=NN):
    return lax.dot_general(lhs, rhs, dims, preferred_element_type=F32)


def product(lhs, rhs, dims=NN):
    lhs_high, lhs_low = halves(lhs)
    rhs_high, rhs_low = halves(rhs)
    both = jnp.concatenate([lhs_high, lhs_low], axis=1)
    twice = jnp.concatenate([rhs_high, rhs_high], axis=1 if dims is NT else 0)
    return dot(both, twice, dims) + dot(lhs_high, rhs_low, dims)


def split_dot(lhs, rhs):
    return dot(lhs[0], rhs[0]) + (dot(lhs[0], rhs[1]) + dot(lhs[1], rhs[0]))


def carry_over(matrix, env, source):
    return product(product(matrix, env), matrix, NT) + source


def fold(value):
    return jnp.sum(value.reshape(-1, 8, BLK), axis=0)


def remote(src, dst, send_sem, recv_sem, device):
    return pltpu.make_async_remote_copy(src, dst, send_sem, recv_sem, device_id=device, device_id_type=MESH)


def update_kernel(v_ref, t_ref, e_ref, c_ref, p_ref, kept_ref, out_ref, energy_ref, left_ref,
                  mine, elements, window, came, far, ends, envs,
                  ghost, ghost_c, vp, w0, r0, w1, w_ghost, t_ghost, crossed,
                  xh, xl, yh, yl, own_a, ghost_a, cross_a, right_w, phys_a, sums,
                  send_a, recv_a, send_z, recv_z, send_e, recv_e,
                  send_v, recv_v, send_w, recv_w, send_t, recv_t, send_p, recv_p):
    chain = lax.axis_index("chain")
    sector = lax.axis_index("sector")
    x = lax.rem(chain, NX)
    z = lax.div(chain, NX)
    odd = lax.rem(x, 2)
    zz = z + odd * (NZ - 1 - 2 * z)
    my_slot = x + odd * (NX - 1 - 2 * x)
    has_below = sector > 0
    has_above = sector < NS - 1
    below = (chain, sector - 1)
    above = (chain, sector + 1)

    def in_row(other):
        return (z * NX + other, sector)

    def in_column(other):
        return ((other + odd * (NZ - 1 - 2 * other)) * NX + x, sector)

    def slot_of(column):
        return x if column % 2 == 0 else NX - 1 - x

    def peer(hop):
        return lax.rem(sector + hop, NS)

    for k in range(2):
        transfer = t_ref[k]
        source = 0.5 * (e_ref[k] + e_ref[k].T)
        mine[2 * k, :BLK] = transfer.T
        mine[2 * k + 1, :BLK] = transfer
        mine[2 * k, BLK:] = source
        mine[2 * k + 1, BLK:] = source
    came[...] = jnp.zeros_like(came)
    far[...] = jnp.zeros_like(far)

    @pl.when(sector == 0)
    def _():
        ghost[0] = jnp.zeros((ROWS, BLK), F32)
        ghost_c[...] = jnp.zeros_like(ghost_c)
        w_ghost[0] = jnp.zeros((PHYS, BLK, BLK), F32)
        t_ghost[1] = jnp.zeros((PAIRS, BLK, BLK), F32)

    @pl.when(sector == NS - 1)
    def _():
        ghost[1] = jnp.zeros((ROWS, BLK), F32)
        w_ghost[1] = jnp.zeros((PHYS, BLK, BLK), F32)
        t_ghost[0] = jnp.zeros((PAIRS, BLK, BLK), F32)

    barrier = pltpu.get_barrier_semaphore()
    greeted = NX - 1 + NS - 1
    for hop in range(1, NX):
        pl.semaphore_signal(barrier, inc=1, device_id=in_row(lax.rem(x + hop, NX)), device_id_type=MESH)
    for hop in range(1, NS):
        pl.semaphore_signal(barrier, inc=1, device_id=(chain, peer(hop)), device_id_type=MESH)
    for hop in (1, 2, 5):
        for other, there in ((zz + hop, zz + hop < NZ), (zz - hop, zz >= hop)):
            @pl.when(there)
            def _():
                pl.semaphore_signal(barrier, inc=1, device_id=in_column(other), device_id_type=MESH)
            greeted = greeted + there.astype(jnp.int32)
    pl.semaphore_wait(barrier, greeted)

    def spread(at, parts):
        rows = [jnp.sum(part, axis=0, keepdims=True) for part in parts]
        rows += [jnp.zeros((1, BLK), F32)] * (8 - len(rows))
        sums[at, pl.ds(sector, 1)] = jnp.concatenate(rows, axis=0)[None]
        for hop in range(1, NS):
            remote(sums.at[at, sector], sums.at[at, sector], send_p.at[at, hop], recv_p.at[at, sector],
                   (chain, peer(hop))).start()

    def collect(at, count):
        for hop in range(1, NS):
            other = peer(hop)
            remote(sums.at[at, other], sums.at[at, other], send_p.at[at, hop], recv_p.at[at, other],
                   (chain, other)).wait_recv()
        total = sums[at, 0]
        for other in range(1, NS):
            total = total + sums[at, other]
        total = jnp.sum(total, axis=1, keepdims=True)
        return [total[i:i + 1] for i in range(count)]

    def deal(column):
        slot = slot_of(column)
        return remote(mine.at[column], elements.at[slot], send_a.at[column], recv_a.at[slot], in_row(column))

    for column in range(NX):
        @pl.when(x != column)
        def _():
            deal(column).start()
    elements[pl.ds(my_slot, 1)] = mine[pl.ds(x, 1)]

    def ghost_up():
        return remote(v_ref.at[1], ghost.at[0], send_v.at[0], recv_v.at[0], above)

    def ghost_down():
        return remote(v_ref.at[0], ghost.at[1], send_v.at[1], recv_v.at[1], below)

    def coupling_up():
        return remote(c_ref.at[1], ghost_c, send_v.at[2], recv_v.at[2], above)

    @pl.when(has_above)
    def _():
        coupling_up().start()
        ghost_up().start()

    @pl.when(has_below)
    def _():
        ghost_down().start()

    def square(i, total):
        part = v_ref[:, pl.ds(pl.multiple_of(i * 256, 256), 256), :]
        return total + fold(part * part)

    spread(0, [lax.fori_loop(0, 8, square, jnp.zeros((8, BLK), F32))])

    for slot in range(NX):
        @pl.when(my_slot != slot)
        def _():
            remote(mine.at[slot], elements.at[slot], send_a.at[slot], recv_a.at[slot],
                   in_row(lax.rem(x + 1, NX))).wait_recv()

    q0, q1, q2, q3 = [elements[s, :BLK] for s in range(NX)]
    s0, s1, s2, s3 = [elements[s, BLK:] for s in range(NX)]
    q01 = product(q1, q0)
    y01 = carry_over(q1, s0, s1)
    q23 = product(q3, q2)
    y23 = carry_over(q3, s2, s3)
    qw = product(q23, q01)
    yw = carry_over(q23, y01, y23)

    def step(at, hop):
        return remote(window.at[at], came.at[at], send_z.at[at], recv_z.at[at], in_column(zz + hop))

    def receive(at, hop):
        @pl.when(zz >= hop)
        def _():
            remote(window.at[at], came.at[at], send_z.at[at], recv_z.at[at], in_column(zz - hop)).wait_recv()

    def start_wave():
        inverse = 1.0 / jnp.sqrt(collect(0, 1)[0])
        inverses = jnp.broadcast_to(inverse, (BLK, BLK))

        def one(p, carry):
            for k in range(2):
                value = v_ref[k, pl.ds(p, BLK, stride=PHYS), :] * inverses
                vp[k, p] = value
                high, low = halves(value)
                xh[p, BLK * (k + 1):BLK * (k + 2), :] = high
                xl[p, BLK * (k + 1):BLK * (k + 2), :] = low
            return carry

        lax.fori_loop(0, PHYS, one, 0)
        return inverses

    def make_phys():
        sym = 0.5 * (p_ref[...] + p_ref[...].T)
        lane = lax.broadcasted_iota(jnp.int32, (PHYS, 256), 1)
        row = lax.broadcasted_iota(jnp.int32, (PHYS, 256), 0)
        spread_p = (lax.div(lane, PHYS) == row).astype(BF16)
        same = (lax.rem(lane, PHYS) == row).astype(F32)
        for i, half in enumerate(halves(sym)):
            wide = dot(half, spread_p)
            for p in range(PHYS):
                phys_a[i, PHYS * p:PHYS * (p + 1), :] = (wide[p:p + 1, :] * same).astype(BF16)

    def phys_piece(high, low, k, i):
        first = pl.multiple_of(BLK * (k + 1) + 32 * i, 32)
        second = pl.multiple_of(BLK * (k + 1) + 32 * i + 16, 16)
        rhs = [jnp.concatenate([
            jnp.concatenate([ref[p, pl.ds(at, 16), :] for p in range(PHYS)], axis=0)
            for at in (first, second)], axis=1) for ref in (high, low)]
        return split_dot((phys_a[0], phys_a[1]), rhs)

    def phys_product(high, low, dst):
        def one(i, carry):
            for k in range(2):
                value = phys_piece(high, low, k, i)
                at = pl.multiple_of(32 * i, 32)
                for p in range(PHYS):
                    rows = value[PHYS * p:PHYS * (p + 1)]
                    dst[k, p, pl.ds(at, 32), :] = jnp.concatenate([rows[:, :BLK], rows[:, BLK:]], axis=0)
            return carry

        lax.fori_loop(0, BLK // 32, one, 0)

    def make_ghost_matrices():
        zero = jnp.zeros((BLK, BLK), BF16)
        from_below = halves(ghost_c[...])
        from_above = halves(c_ref[1].T)
        up = halves(c_ref[1])
        down = halves(ghost_c[...].T)
        for i in range(2):
            ghost_a[i] = jnp.concatenate([jnp.concatenate([from_below[i], zero], axis=1),
                                          jnp.concatenate([zero, from_above[i]], axis=1)], axis=0)
            cross_a[i] = jnp.concatenate([jnp.concatenate([up[i], zero], axis=1),
                                          jnp.concatenate([zero, down[i]], axis=1)], axis=0)

    def ghost_halves(i, low, high):
        p = 2 * i
        parts = [halves(jnp.concatenate([low(p + j), high(p + j)], axis=0)) for j in range(2)]
        return [jnp.concatenate([parts[0][h], parts[1][h]], axis=1) for h in range(2)]

    def add_ghosts(inverses):
        def one(i, carry):
            rhs = ghost_halves(i, lambda p: ghost[0, pl.ds(p, BLK, stride=PHYS), :] * inverses,
                               lambda p: ghost[1, pl.ds(p, BLK, stride=PHYS), :] * inverses)
            value = split_dot((ghost_a[0], ghost_a[1]), rhs)
            for k in range(2):
                for j in range(2):
                    w0[k, 2 * i + j] = w0[k, 2 * i + j] + value[BLK * k:BLK * (k + 1), BLK * j:BLK * (j + 1)]
            return carry

        lax.fori_loop(0, PAIRS, one, 0)

    for at, hop in ((0, 1), (1, 2)):
        window[at, :BLK] = qw
        window[at, BLK:] = yw
        @pl.when(zz + hop < NZ)
        def _():
            step(at, hop).start()
        if at == 0:
            q012 = product(q2, q01)
            y012 = carry_over(q2, y01, s2)
            inverses = start_wave()
            make_phys()
        else:
            phys_product(xh, xl, w0)
        receive(at, hop)
        qp, yp = came[at, :BLK], came[at, BLK:]
        qn = product(qw, qp)
        yw = carry_over(qw, yp, yw)
        qw = qn

    window[2, :BLK] = qw
    window[2, BLK:] = yw
    far_copy = remote(window.at[2, pl.ds(BLK, BLK)], far, send_z.at[3], recv_z.at[3], in_column(zz + 5))

    @pl.when(zz + 1 < NZ)
    def _():
        step(2, 1).start()

    @pl.when(zz + 5 < NZ)
    def _():
        far_copy.start()

    @pl.when(has_below)
    def _():
        coupling_up().wait_recv()
        ghost_up().wait_recv()

    @pl.when(has_above)
    def _():
        ghost_down().wait_recv()

    make_ghost_matrices()
    add_ghosts(inverses)

    @pl.when(zz >= 5)
    def _():
        remote(window.at[2, pl.ds(BLK, BLK)], far, send_z.at[3], recv_z.at[3], in_column(zz - 5)).wait_recv()
    receive(2, 1)
    start = carry_over(came[2, :BLK], far[...], came[2, BLK:])

    def owner(slot):
        return slot + odd * (NX - 1 - 2 * slot)

    def give(slot):
        return remote(ends.at[slot], envs.at[x], send_e.at[slot], recv_e.at[x], in_row(owner(slot)))

    for slot, (q, y) in enumerate(((None, None), (q0, s0), (q01, y01), (q012, y012))):
        ends[slot] = start if slot == 0 else carry_over(q, start, y)
        @pl.when(my_slot != slot)
        def _():
            give(slot).start()
    envs[pl.ds(x, 1)] = ends[pl.ds(my_slot, 1)]
    for column in range(NX):
        @pl.when(x != column)
        def _():
            remote(ends.at[column], envs.at[column], send_e.at[column], recv_e.at[column], in_row(column)).wait_recv()

    for k in range(2):
        left_ref[k] = envs[2 * k]
        high, low = halves(envs[2 * k + 1])
        right_w[k] = jnp.concatenate([jnp.concatenate([high, low], axis=1),
                                      jnp.concatenate([high, jnp.zeros_like(low)], axis=1)], axis=0)
    own = halves(jnp.concatenate([jnp.concatenate([envs[0], c_ref[0].T], axis=1),
                                  jnp.concatenate([c_ref[0], envs[2]], axis=1)], axis=0))
    own_a[0] = own[0]
    own_a[1] = own[1]

    def own_product(high, low, i):
        p = 2 * i
        hs = [high[p + j, BLK:3 * BLK, :] for j in range(2)]
        ls = [low[p + j, BLK:3 * BLK, :] for j in range(2)]
        left = split_dot((own_a[0], own_a[1]), (jnp.concatenate(hs, axis=1), jnp.concatenate(ls, axis=1)))
        blocks = []
        for k in range(2):
            rows = slice(BLK * k, BLK * (k + 1))
            lhs = jnp.concatenate([jnp.concatenate([h[rows], l[rows]], axis=1) for h, l in zip(hs, ls)], axis=0)
            right = dot(lhs, right_w[k])
            right = right[:, :BLK] + right[:, BLK:]
            blocks.append([left[rows, BLK * j:BLK * (j + 1)] + right[BLK * j:BLK * (j + 1)] for j in range(2)])
        return blocks

    def wave_down(part):
        at = pl.ds(part * CHUNK, CHUNK)
        return remote(w0.at[0, at], w_ghost.at[1, at], send_w.at[1, part], recv_w.at[1, part], below)

    def wave_up(part):
        at = pl.ds(part * CHUNK, CHUNK)
        return remote(w0.at[1, at], w_ghost.at[0, at], send_w.at[0, part], recv_w.at[0, part], above)

    def first_apply(i, total):
        blocks = own_product(xh, xl, i)
        for k in range(2):
            for j in range(2):
                p = 2 * i + j
                value = w0[k, p] + blocks[k][j]
                w0[k, p] = value
                high, low = halves(value)
                yh[p, BLK * (k + 1):BLK * (k + 2), :] = high
                yl[p, BLK * (k + 1):BLK * (k + 2), :] = low
                total = total + fold(value * vp[k, p])
        return total

    zeros = jnp.zeros((8, BLK), F32)
    total = zeros
    for part in range(CHUNKS):
        total = lax.fori_loop(part * CHUNK // 2, (part + 1) * CHUNK // 2, first_apply, total)

        @pl.when(has_below)
        def _():
            wave_down(part).start()

        @pl.when(has_above)
        def _():
            wave_up(part).start()
    spread(1, [total])

    phys_product(yh, yl, w1)

    def second_apply(i, carry):
        blocks = own_product(yh, yl, i)
        for k in range(2):
            for j in range(2):
                w1[k, 2 * i + j] = w1[k, 2 * i + j] + blocks[k][j]
        return carry

    lax.fori_loop(0, PAIRS, second_apply, 0)
    corr = collect(1, 1)[0]
    corrs = jnp.broadcast_to(corr, (BLK, BLK))

    def finish(i, totals):
        rr, w0r, rt, vt, w0t, tt = totals
        rhs = ghost_halves(i, lambda p: w_ghost[0, p], lambda p: w_ghost[1, p])
        value = split_dot((ghost_a[0], ghost_a[1]), rhs)
        for k in range(2):
            for j in range(2):
                p = 2 * i + j
                applied = w0[k, p]
                wave = vp[k, p]
                residual = applied - corrs * wave
                turned = w1[k, p] + value[BLK * k:BLK * (k + 1), BLK * j:BLK * (j + 1)] - corrs * applied
                r0[k, p] = residual
                w1[k, p] = turned
                high, low = halves(turned)
                xh[p, BLK * (k + 1):BLK * (k + 2), :] = high
                xl[p, BLK * (k + 1):BLK * (k + 2), :] = low
                rr = rr + fold(residual * residual)
                w0r = w0r + fold(applied * residual)
                rt = rt + fold(residual * turned)
                vt = vt + fold(wave * turned)
                w0t = w0t + fold(applied * turned)
                tt = tt + fold(turned * turned)
        return rr, w0r, rt, vt, w0t, tt

    def turned_down(part):
        at = pl.ds(part * CHUNK, CHUNK)
        return remote(w1.at[0, at], t_ghost.at[0, at], send_t.at[part], recv_t.at[part], below)

    def turned_up(part):
        at = pl.ds(part * CHUNK, CHUNK)
        to = pl.ds(part * CHUNK - PAIRS, CHUNK)
        return remote(w1.at[1, at], t_ghost.at[1, to], send_t.at[part], recv_t.at[part], above)

    totals = (zeros,) * 6
    for part in range(CHUNKS):
        @pl.when(has_below)
        def _():
            wave_up(part).wait_recv()

        @pl.when(has_above)
        def _():
            wave_down(part).wait_recv()

        totals = lax.fori_loop(part * CHUNK // 2, (part + 1) * CHUNK // 2, finish, totals)
        if part < CHUNKS // 2:
            @pl.when(has_below)
            def _():
                turned_down(part).start()
        else:
            @pl.when(has_above)
            def _():
                turned_up(part).start()
    w0t, tt = totals[4:]
    spread(2, list(totals[:4]))

    def third_apply(i, total):
        blocks = own_product(xh, xl, i)
        for k in range(2):
            for j in range(2):
                total = total + fold(blocks[k][j] * w1[k, 2 * i + j])
        return total

    def third_phys(i, total):
        for k in range(2):
            value = phys_piece(xh, xl, k, i)
            at = pl.multiple_of(32 * i, 32)
            for p in range(PHYS):
                rows = value[PHYS * p:PHYS * (p + 1)]
                both = jnp.concatenate([rows[:, :BLK], rows[:, BLK:]], axis=0)
                total = total + fold(both * w1[k, p, pl.ds(at, 32), :])
        return total

    def cross(i, carry):
        p = 2 * i
        rhs = [jnp.concatenate([
            jnp.concatenate([ref[p + j, 2 * BLK:3 * BLK, :], ref[p + PAIRS + j, BLK:2 * BLK, :]], axis=0)
            for j in range(2)], axis=1) for ref in (xh, xl)]
        value = split_dot((cross_a[0], cross_a[1]), rhs)
        for side in range(2):
            for j in range(2):
                crossed[side, p + j] = value[BLK * side:BLK * (side + 1), BLK * j:BLK * (j + 1)]
        return carry

    lax.fori_loop(0, PAIRS // 2, cross, 0)
    tht = lax.fori_loop(0, PAIRS, third_apply, zeros)
    tht = lax.fori_loop(0, BLK // 32, third_phys, tht)

    rr, w0r, rt, vt = collect(2, 4)
    norm = jnp.sqrt(rr + EPS)
    curvature = rt / (rr + EPS)
    coupled = w0r / norm
    ritz = 0.5 * (corr + curvature) - jnp.sqrt(0.25 * (corr - curvature) ** 2 + coupled * coupled)
    coef = ritz - corr
    magnitude = jnp.sqrt(coupled * coupled + coef * coef)
    wave_v = coupled / magnitude
    wave_r = coef / (magnitude * norm)
    corr2 = wave_v * wave_v * corr + wave_v * wave_r * (vt + w0r) + wave_r * wave_r * rt
    res_v = wave_v * (corr - corr2)
    res_r = wave_v - corr2 * wave_r
    res_t = wave_r

    masks = [(lax.broadcasted_iota(jnp.int32, (1, BLK), 1) < kept_ref[0, k]).astype(F32) for k in range(2)]
    wide = [jnp.broadcast_to(value, (BLK, BLK)) for value in (wave_v, wave_r, wave_v * corr, res_v, res_r, res_t)]

    def second_residual(p, totals):
        rr2, ar2, mww, mwr, mrr = totals
        for k in range(2):
            wave, residual, turned = vp[k, p], r0[k, p], w1[k, p]
            now = wide[0] * wave + wide[1] * residual
            applied = wide[2] * wave + wide[0] * residual + wide[1] * turned
            second = wide[3] * wave + wide[4] * residual + wide[5] * turned
            rr2 = rr2 + fold(second * second)
            ar2 = ar2 + fold(applied * second)
            mww = mww + masks[k] * fold(now * now)
            mwr = mwr + masks[k] * fold(now * second)
            mrr = mrr + masks[k] * fold(second * second)
        return rr2, ar2, mww, mwr, mrr

    finals = lax.fori_loop(0, PHYS, second_residual, (zeros,) * 5)

    for part in range(CHUNKS):
        if part < CHUNKS // 2:
            @pl.when(has_above)
            def _():
                turned_down(part).wait_recv()
        else:
            @pl.when(has_below)
            def _():
                turned_up(part).wait_recv()

    def meet(i, total):
        return total + fold(crossed[0, i] * t_ghost[0, i]) + fold(crossed[1, i] * t_ghost[1, i])

    tht = tht + 2.0 * lax.fori_loop(0, PAIRS, meet, zeros)
    spread(3, list(finals) + [tht, w0t, tt])
    rr2, ar2, mww, mwr, mrr, tht, w0t, tt = collect(3, 8)
    norm2 = jnp.sqrt(rr2 + EPS)
    turned2 = (res_v * res_v * corr + res_r * res_r * rt + res_t * res_t * tht
               + 2.0 * (res_v * res_r * vt + res_v * res_t * w0t + res_r * res_t * tt))
    curvature = turned2 / (rr2 + EPS)
    coupled = ar2 / norm2
    ritz = 0.5 * (corr2 + curvature) - jnp.sqrt(0.25 * (corr2 - curvature) ** 2 + coupled * coupled)
    coef = ritz - corr2
    magnitude = jnp.sqrt(coupled * coupled + coef * coef)
    of_wave = coupled / magnitude
    of_res = coef / (magnitude * norm2)
    kept = of_wave * of_wave * mww + 2.0 * of_wave * of_res * mwr + of_res * of_res * mrr
    scale = 1.0 / jnp.sqrt(kept + EPS)
    energy_ref[...] = jnp.broadcast_to(ritz, (8, BLK))
    last = [jnp.broadcast_to(scale * value, (BLK, BLK)) for value in (
        of_wave * wave_v + of_res * res_v, of_wave * wave_r + of_res * res_r, of_res * res_t)]

    def write(p, carry):
        for k in range(2):
            value = last[0] * vp[k, p] + last[1] * r0[k, p] + last[2] * w1[k, p]
            out_ref[k, pl.ds(p, BLK, stride=PHYS), :] = value * masks[k]
        return carry

    lax.fori_loop(0, PHYS, write, 0)

    for column in range(NX):
        @pl.when(x != column)
        def _():
            deal(column).wait_send()
    for at, hop in ((0, 1), (1, 2), (2, 1)):
        @pl.when(zz + hop < NZ)
        def _():
            step(at, hop).wait_send()
    @pl.when(zz + 5 < NZ)
    def _():
        far_copy.wait_send()
    for slot in range(NX):
        @pl.when(my_slot != slot)
        def _():
            give(slot).wait_send()
    for at in range(4):
        for hop in range(1, NS):
            remote(sums.at[at, sector], sums.at[at, sector], send_p.at[at, hop], recv_p.at[at, sector],
                   (chain, peer(hop))).wait_send()

    @pl.when(has_above)
    def _():
        coupling_up().wait_send()
        ghost_up().wait_send()
        for part in range(CHUNKS):
            wave_up(part).wait_send()
            if part >= CHUNKS // 2:
                turned_up(part).wait_send()

    @pl.when(has_below)
    def _():
        ghost_down().wait_send()
        for part in range(CHUNKS):
            wave_down(part).wait_send()
            if part < CHUNKS // 2:
                turned_down(part).wait_send()


def per_device(wave_start, transfer, energy_terms, coupling, physical, kept_ranks):
    vmem = pl.BlockSpec(memory_space=pltpu.VMEM)
    dma = pltpu.SemaphoreType.DMA
    out, energy, left = pl.pallas_call(
        update_kernel,
        out_shape=(
            jax.ShapeDtypeStruct((2, ROWS, BLK), F32),
            jax.ShapeDtypeStruct((8, BLK), F32),
            jax.ShapeDtypeStruct((2, BLK, BLK), F32),
        ),
        in_specs=[vmem] * 5 + [pl.BlockSpec(memory_space=pltpu.SMEM)],
        out_specs=(vmem, vmem, vmem),
        scratch_shapes=[
            pltpu.VMEM((NX, 2 * BLK, BLK), F32),
            pltpu.VMEM((NX, 2 * BLK, BLK), F32),
            pltpu.VMEM((3, 2 * BLK, BLK), F32),
            pltpu.VMEM((3, 2 * BLK, BLK), F32),
            pltpu.VMEM((BLK, BLK), F32),
            pltpu.VMEM((NX, BLK, BLK), F32),
            pltpu.VMEM((NX, BLK, BLK), F32),
            pltpu.VMEM((2, ROWS, BLK), F32),
            pltpu.VMEM((BLK, BLK), F32),
            pltpu.VMEM((2, PHYS, BLK, BLK), F32),
            pltpu.VMEM((2, PHYS, BLK, BLK), F32),
            pltpu.VMEM((2, PHYS, BLK, BLK), F32),
            pltpu.VMEM((2, PHYS, BLK, BLK), F32),
            pltpu.VMEM((2, PHYS, BLK, BLK), F32),
            pltpu.VMEM((2, PAIRS, BLK, BLK), F32),
            pltpu.VMEM((2, PAIRS, BLK, BLK), F32),
            pltpu.VMEM((PHYS, 4 * BLK, BLK), BF16),
            pltpu.VMEM((PHYS, 4 * BLK, BLK), BF16),
            pltpu.VMEM((PHYS, 4 * BLK, BLK), BF16),
            pltpu.VMEM((PHYS, 4 * BLK, BLK), BF16),
            pltpu.VMEM((2, 2 * BLK, 2 * BLK), BF16),
            pltpu.VMEM((2, 2 * BLK, 2 * BLK), BF16),
            pltpu.VMEM((2, 2 * BLK, 2 * BLK), BF16),
            pltpu.VMEM((2, 2 * BLK, 2 * BLK), BF16),
            pltpu.VMEM((2, 2 * BLK, 2 * BLK), BF16),
            pltpu.VMEM((4, NS, 8, BLK), F32),
            dma((NX,)), dma((NX,)), dma((4,)), dma((4,)), dma((NX,)), dma((NX,)),
            dma((3,)), dma((3,)), dma((2, CHUNKS)), dma((2, CHUNKS)), dma((CHUNKS,)), dma((CHUNKS,)),
            dma((4, NS)), dma((4, NS)),
        ],
        compiler_params=pltpu.CompilerParams(
            collective_id=0, has_side_effects=True, vmem_limit_bytes=52 << 20),
    )(wave_start.reshape(2, ROWS, BLK), transfer[0], energy_terms[0], coupling[0], physical[0], kept_ranks)
    return (out.reshape(wave_start.shape), energy[0, :1], left[None])


def solution(mesh):
    placed = (
        P("chain", "sector", None, None, None),
        P("chain", "sector", None, None),
        P("chain", "sector", None, None),
        P("chain", "sector", None, None),
        P("chain", None, None),
        P("chain", "sector"),
    )
    return jax.shard_map(
        per_device,
        mesh=mesh,
        in_specs=placed,
        out_specs=(
            P("chain", "sector", None, None, None),
            P("chain"),
            P("chain", "sector", None, None),
        ),
        check_vma=False,
    )
```

time: 279 us -> 88.8 us (0.32); the launches traced: 275 us -> 88.5 us
  blocking collectives: 111 us -> 0 us
  matrix products: 44.5 us -> 0 us
  Pallas kernels: 36 us -> 79.6 us
  other arithmetic: 34.1 us -> 0 us
  starting transfers between devices: 14.4 us -> 0 us
  between operations: 14.2 us -> 0.65 us
  waiting for transfers between devices: 13.3 us -> 0 us
    psum x8 -> x0, blocking collectives: 111 us -> none  [the longest x2 33.4 us: per_device(): correlation = lax.psum(jnp.sum(wave * applied), 'sector')]
    dot_general x15 -> x0, matrix products: 44.5 us -> none  [the longest x3 16.1 us: apply_products(): lowered = jnp.einsum('kba,kbpc->kapc', coupler, above, precision=HIGHEST)]
    pallas_call x1, Pallas kernels: 36 us -> 79.6 us  [per_device(): pl.pallas_call(update_kernel, out_shape=(jax.ShapeDtypeStruct((2, ROWS, B...]
    reduce_sum x6 -> x0, other arithmetic: 25.1 us -> none  [the longest x2 7.57 us: per_device(): res_norm = lax.psum(jnp.sum(residual * residual), 'sector')]
    ppermute x6 -> x0, starting transfers between devices: 14.4 us -> none  [shifted(): return lax.ppermute(block, axis, route)]
    ppermute x6 -> x0, waiting for transfers between devices: 13.3 us -> none  [shifted(): return lax.ppermute(block, axis, route)]
    div x3 -> x0, other arithmetic: 6.23 us -> none  [the longest x1 3.59 us: per_device(): unit_dir = residual / jnp.sqrt(res_norm + EPS)]
    unnamed x22 -> x12, local copies, waits for them, and re-layouts: 3.25 us -> 7.75 us
  transfers between devices with their start and end apart: 6 -> 0, of which waited for: 4 -> 0; matrix products, arithmetic and copies ran while one was open for 9% -> 0% of each run, Pallas kernels for 13% -> 0%
where the time goes in v2:
time: 88.8 us; the launch traced here: 88.5 us
  Pallas kernels  79.6 us (90%)
  local copies, waits for them, and re-layouts  8.27 us (9%)
    pallas_call x1, Pallas kernels, per_device(): pl.pallas_call(update_kernel, out_shape=(jax.ShapeDtypeStruct((2, ROWS, B...  79.6 us
    unnamed x12, local copies, waits for them, and re-layouts  7.75 us

profile of v2, /device:TPU:1, one launch (start us, length us, event | category | flops | bytes accessed | tf_op | source)
XLA Modules:
  0.0 88.5 jit_solution(4317468730740255255)
XLA Ops:
  0.6 0.0 copy-start
  0.6 0.9 %copy-done = f32[1,2,128,128]{3,2,1,0:T(8,128)S(1)} copy-done((f32[1,2,128,128]{3,2,1,0:T(8,128)S(1)}, f32[1,2,128,128]{3,2,1,0:T(8,128)}, u32[]{:S(2)}) %copy-start) | copy-done | bytes 131096
  1.5 0.0 copy-start.1
  1.5 0.9 %copy-done.1 = f32[1,2,128,128]{3,2,1,0:T(8,128)S(1)} copy-done((f32[1,2,128,128]{3,2,1,0:T(8,128)S(1)}, f32[1,2,128,128]{3,2,1,0:T(8,128)}, u32[]{:S(2)}) %copy-start.1) | copy-done | bytes 131096
  2.4 0.0 copy-start.2
  2.4 0.9 %copy-done.2 = f32[1,2,128,128]{3,2,1,0:T(8,128)S(1)} copy-done((f32[1,2,128,128]{3,2,1,0:T(8,128)S(1)}, f32[1,2,128,128]{3,2,1,0:T(8,128)}, u32[]{:S(2)}) %copy-start.2) | copy-done | bytes 131096
  3.3 0.0 copy-start.3
  3.3 0.7 copy-done.3
  4.0 0.0 copy-start.4
  4.0 0.7 copy-done.4
  4.7 79.6 %shard_map.85 = (f32[2,2048,128]{2,1,0:T(8,128)}, f32[8,128]{1,0:T(8,128)S(1)}, f32[2,128,128]{2,1,0:T(8,128)S(1)}) custom-call(f32[2,2048,128]{2,1,0:T(8,128)} %bitcast.13, f32[2,128,128]{2,1,0:T(8,128)S(1)} %bitcast.8, f32[2,128,128]{2,1,0:T(8,128)S(1)} %bitcast.9, f32[2,128,128]{2,1,0:T(8,128)S(1)} %bitcast.10, f32[16,16]{1,0:T(8,128)S(1)} %bitcast.12, ...), custom_call_target="tpu_custom_call" | custom-call | tf_op jit(solution)/shard_map/pallas_call | solution.py:619
  84.3 0.5 slice.3
  84.8 3.0 %copy.11 = f32[1,2,128,16,128]{4,3,2,1,0:T(8,128)} copy(f32[1,2,128,16,128]{4,3,2,1,0:T(8,128)} %bitcast.14) | data formatting | bytes 4194304
  87.9 0.7 copy.12
Async XLA Ops:
  0.6 0.9 %copy-start = (f32[1,2,128,128]{3,2,1,0:T(8,128)S(1)}, f32[1,2,128,128]{3,2,1,0:T(8,128)}, u32[]{:S(2)}) copy-start(f32[1,2,128,128]{3,2,1,0:T(8,128)} %param.7) | copy-start | bytes 393220
  1.5 0.9 %copy-start.1 = (f32[1,2,128,128]{3,2,1,0:T(8,128)S(1)}, f32[1,2,128,128]{3,2,1,0:T(8,128)}, u32[]{:S(2)}) copy-start(f32[1,2,128,128]{3,2,1,0:T(8,128)} %param.8) | copy-start | bytes 393220
  2.4 0.9 %copy-start.2 = (f32[1,2,128,128]{3,2,1,0:T(8,128)S(1)}, f32[1,2,128,128]{3,2,1,0:T(8,128)}, u32[]{:S(2)}) copy-start(f32[1,2,128,128]{3,2,1,0:T(8,128)} %param.9) | copy-start | bytes 393220
  3.3 0.7 copy-start.3
  4.0 0.7 copy-start.4

commit v3 on v2

v3 whole, which is shorter than its diff:
```python
import functools

import jax
import jax.numpy as jnp
from jax import lax
from jax.experimental import pallas as pl
from jax.experimental.pallas import tpu as pltpu
from jax.sharding import PartitionSpec as P

BLK = 128
PHYS = 16
NX = 4
NZ = 8
NS = 8
ROWS = BLK * PHYS
CHUNKS = 4
CHUNK = PHYS // CHUNKS
PAIRS = PHYS // 2

EPS = 1e-06
MESH = pl.DeviceIdType.MESH
F32 = jnp.float32
BF16 = jnp.bfloat16
NN = (((1,), (0,)), ((), ()))
NT = (((1,), (1,)), ((), ()))


def halves(value):
    high = value.astype(BF16)
    return high, (value - high.astype(F32)).astype(BF16)


def dot(lhs, rhs, dims=NN):
    return lax.dot_general(lhs, rhs, dims, preferred_element_type=F32)


def product(lhs, rhs, dims=NN):
    lhs_high, lhs_low = halves(lhs)
    rhs_high, rhs_low = halves(rhs)
    both = jnp.concatenate([lhs_high, lhs_low], axis=1)
    twice = jnp.concatenate([rhs_high, rhs_high], axis=1 if dims is NT else 0)
    return dot(both, twice, dims) + dot(lhs_high, rhs_low, dims)


def split_dot(lhs, rhs):
    return dot(lhs[0], rhs[0]) + (dot(lhs[0], rhs[1]) + dot(lhs[1], rhs[0]))


def carry_over(matrix, env, source):
    return product(product(matrix, env), matrix, NT) + source


def fold(value):
    return jnp.sum(value.reshape(-1, 8, BLK), axis=0)


def remote(src, dst, send_sem, recv_sem, device):
    return pltpu.make_async_remote_copy(src, dst, send_sem, recv_sem, device_id=device, device_id_type=MESH)


def update_kernel(v_hbm, t_hbm, e_hbm, c_hbm, p_hbm, kept_hbm, out_ref, energy_ref, left_ref,
                  v_ref, t_ref, e_ref, c_ref, p_ref, kept_ref,
                  mine, elements, window, came, far, partial, ends, envs,
                  ghost, ghost_c, vp, w0, r0, w1, w_ghost, t_ghost, lr_ghost, crossed,
                  xh, xl, yh, yl, own_l, own_a, ghost_a, cross_a, ghost_l, right_w, phys_a, sums,
                  load, send_a, recv_a, send_z, recv_z, send_f, recv_f, send_e, recv_e,
                  send_v, recv_v, send_w, recv_w, send_t, recv_t, send_p, recv_p):
    chain = lax.axis_index("chain")
    sector = lax.axis_index("sector")
    x = lax.rem(chain, NX)
    z = lax.div(chain, NX)
    odd = lax.rem(x, 2)
    zz = z + odd * (NZ - 1 - 2 * z)
    my_slot = x + odd * (NX - 1 - 2 * x)
    has_below = sector > 0
    has_above = sector < NS - 1
    below = (chain, sector - 1)
    above = (chain, sector + 1)

    def in_row(other):
        return (z * NX + other, sector)

    def in_column(other):
        return ((other + odd * (NZ - 1 - 2 * other)) * NX + x, sector)

    def slot_of(column):
        return x if column % 2 == 0 else NX - 1 - x

    def peer(hop):
        return lax.rem(sector + hop, NS)

    loads = [pltpu.make_async_copy(src, dst, load.at[i]) for i, (src, dst) in enumerate((
        (t_hbm, t_ref), (e_hbm, e_ref), (v_hbm, v_ref), (c_hbm, c_ref), (p_hbm, p_ref),
        (kept_hbm, kept_ref)))]
    for copy in loads:
        copy.start()

    barrier = pltpu.get_barrier_semaphore()
    greeted = NX - 1 + NS - 1
    for hop in range(1, NX):
        pl.semaphore_signal(barrier, inc=1, device_id=in_row(lax.rem(x + hop, NX)), device_id_type=MESH)
    for hop in range(1, NS):
        pl.semaphore_signal(barrier, inc=1, device_id=(chain, peer(hop)), device_id_type=MESH)
    for hop in (1, 2, 5):
        for other, there in ((zz + hop, zz + hop < NZ), (zz - hop, zz >= hop)):
            @pl.when(there)
            def _():
                pl.semaphore_signal(barrier, inc=1, device_id=in_column(other), device_id_type=MESH)
            greeted = greeted + there.astype(jnp.int32)

    loads[0].wait()
    loads[1].wait()
    for k in range(2):
        transfer = t_ref[k]
        source = 0.5 * (e_ref[k] + e_ref[k].T)
        mine[2 * k, 0] = transfer.T
        mine[2 * k + 1, 0] = transfer
        mine[2 * k, 1] = source
        mine[2 * k + 1, 1] = source
    pl.semaphore_wait(barrier, greeted)

    def spread(at, parts):
        rows = [jnp.sum(part, axis=0, keepdims=True) for part in parts]
        rows += [jnp.zeros((1, BLK), F32)] * (8 - len(rows))
        sums[at, pl.ds(sector, 1)] = jnp.concatenate(rows, axis=0)[None]
        for hop in range(1, NS):
            remote(sums.at[at, sector], sums.at[at, sector], send_p.at[at, hop], recv_p.at[at, sector],
                   (chain, peer(hop))).start()

    def collect(at, count):
        for hop in range(1, NS):
            other = peer(hop)
            remote(sums.at[at, other], sums.at[at, other], send_p.at[at, hop], recv_p.at[at, other],
                   (chain, other)).wait_recv()
        total = sums[at, 0]
        for other in range(1, NS):
            total = total + sums[at, other]
        total = jnp.sum(total, axis=1, keepdims=True)
        return [total[i:i + 1] for i in range(count)]

    def deal(column):
        slot = slot_of(column)
        return remote(mine.at[column], elements.at[slot], send_a.at[column], recv_a.at[slot], in_row(column))

    for hop in (2, 1, 3):
        for column in range(NX):
            @pl.when(column == lax.rem(x + hop, NX))
            def _():
                deal(column).start()
    elements[pl.ds(my_slot, 1)] = mine[pl.ds(x, 1)]

    def ghost_up():
        return remote(v_hbm.at[1], ghost.at[0], send_v.at[0], recv_v.at[0], above)

    def ghost_down():
        return remote(v_hbm.at[0], ghost.at[1], send_v.at[1], recv_v.at[1], below)

    def coupling_up():
        return remote(c_hbm.at[1], ghost_c, send_v.at[2], recv_v.at[2], above)

    @pl.when(has_above)
    def _():
        coupling_up().start()
        ghost_up().start()

    @pl.when(has_below)
    def _():
        ghost_down().start()

    def square(i, total):
        part = v_ref[:, pl.ds(pl.multiple_of(i * 256, 256), 256), :]
        return total + fold(part * part)

    loads[2].wait()
    spread(0, [lax.fori_loop(0, 8, square, jnp.zeros((8, BLK), F32))])

    square_zero = jnp.zeros((BLK, BLK), F32)
    for ref, unused in (
            (came.at[0, 0], (zz < 2) | (zz == NZ - 1)), (came.at[0, 1], (zz < 1) | (zz == NZ - 1)),
            (came.at[1, 0], (zz < 4) | (zz == NZ - 1)), (came.at[1, 1], (zz < 2) | (zz == NZ - 1)),
            (came.at[2, 0], zz < 5), (came.at[2, 1], zz < 1), (far, zz < 5)):
        @pl.when(unused)
        def _():
            ref[...] = square_zero

    @pl.when(sector == 0)
    def _():
        ghost[0] = jnp.zeros((ROWS, BLK), F32)
        ghost_c[...] = square_zero
        w_ghost[0] = jnp.zeros((PHYS, BLK, BLK), F32)
        t_ghost[1] = jnp.zeros((PAIRS, BLK, BLK), F32)
        lr_ghost[0] = jnp.zeros((2, BLK, BLK), F32)

    @pl.when(sector == NS - 1)
    def _():
        ghost[1] = jnp.zeros((ROWS, BLK), F32)
        w_ghost[1] = jnp.zeros((PHYS, BLK, BLK), F32)
        t_ghost[0] = jnp.zeros((PAIRS, BLK, BLK), F32)
        lr_ghost[1] = jnp.zeros((2, BLK, BLK), F32)

    for slot in range(NX):
        @pl.when(my_slot != slot)
        def _():
            remote(mine.at[slot], elements.at[slot], send_a.at[slot], recv_a.at[slot],
                   in_row(lax.rem(x + 1, NX))).wait_recv()

    q0, q1, q2, q3 = [elements[s, 0] for s in range(NX)]
    s0, s1, s2, s3 = [elements[s, 1] for s in range(NX)]
    q01 = product(q1, q0)
    y01 = carry_over(q1, s0, s1)
    q23 = product(q3, q2)
    y23 = carry_over(q3, s2, s3)
    qw = product(q23, q01)
    yw = carry_over(q23, y01, y23)

    hops = (1, 2, 1)
    sends = (((zz >= 1) & (zz <= 5), zz <= 5), ((zz >= 2) & (zz <= 4), zz <= 4), ((zz >= 4) & (zz <= 6), zz <= 6))
    takes = (((zz >= 2) & (zz <= 6), (zz >= 1) & (zz <= 6)), ((zz >= 4) & (zz <= 6), (zz >= 2) & (zz <= 6)),
             (zz >= 5, zz >= 1))

    def step(at, part):
        return remote(window.at[at, part], came.at[at, part], send_z.at[at, part], recv_z.at[at, part],
                      in_column(zz + hops[at]))

    def send(at, part, value):
        window[at, part] = value

        @pl.when(sends[at][part])
        def _():
            step(at, part).start()

    def receive(at, part):
        @pl.when(takes[at][part])
        def _():
            remote(window.at[at, part], came.at[at, part], send_z.at[at, part], recv_z.at[at, part],
                   in_column(zz - hops[at])).wait_recv()
        return came[at, part]

    def far_copy(at):
        return remote(window.at[at, 1], far, send_f.at[0], recv_f.at[0], in_column(zz + 5))

    def send_far(at):
        @pl.when(zz == at)
        def _():
            far_copy(at).start()

    def start_wave():
        inverse = 1.0 / jnp.sqrt(collect(0, 1)[0])
        inverses = jnp.broadcast_to(inverse, (BLK, BLK))

        def one(p, carry):
            for k in range(2):
                value = v_ref[k, pl.ds(p, BLK, stride=PHYS), :] * inverses
                vp[k, p] = value
                high, low = halves(value)
                xh[p, BLK * (k + 1):BLK * (k + 2), :] = high
                xl[p, BLK * (k + 1):BLK * (k + 2), :] = low
            return carry

        lax.fori_loop(0, PHYS, one, 0)
        return inverses

    def make_phys():
        loads[4].wait()
        sym = 0.5 * (p_ref[...] + p_ref[...].T)
        lane = lax.broadcasted_iota(jnp.int32, (PHYS, 256), 1)
        row = lax.broadcasted_iota(jnp.int32, (PHYS, 256), 0)
        spread_p = (lax.div(lane, PHYS) == row).astype(BF16)
        same = (lax.rem(lane, PHYS) == row).astype(F32)
        for i, half in enumerate(halves(sym)):
            wide = dot(half, spread_p)
            for p in range(PHYS):
                phys_a[i, PHYS * p:PHYS * (p + 1), :] = (wide[p:p + 1, :] * same).astype(BF16)

    def phys_piece(high, low, k, i):
        first = pl.multiple_of(BLK * (k + 1) + 32 * i, 32)
        second = pl.multiple_of(BLK * (k + 1) + 32 * i + 16, 16)
        rhs = [jnp.concatenate([
            jnp.concatenate([ref[p, pl.ds(at, 16), :] for p in range(PHYS)], axis=0)
            for at in (first, second)], axis=1) for ref in (high, low)]
        return split_dot((phys_a[0], phys_a[1]), rhs)

    def phys_product(high, low, dst):
        def one(i, carry):
            for k in range(2):
                value = phys_piece(high, low, k, i)
                at = pl.multiple_of(32 * i, 32)
                for p in range(PHYS):
                    rows = value[PHYS * p:PHYS * (p + 1)]
                    dst[k, p, pl.ds(at, 32), :] = jnp.concatenate([rows[:, :BLK], rows[:, BLK:]], axis=0)
            return carry

        lax.fori_loop(0, BLK // 32, one, 0)

    def make_ghost_matrices():
        loads[3].wait()
        zero = jnp.zeros((BLK, BLK), BF16)
        from_below = halves(ghost_c[...])
        from_above = halves(c_ref[1].T)
        up = halves(c_ref[1])
        down = halves(ghost_c[...].T)
        own_up = halves(c_ref[0])
        own_down = halves(c_ref[0].T)
        for i in range(2):
            own_a[i] = jnp.concatenate([jnp.concatenate([zero, own_down[i]], axis=1),
                                        jnp.concatenate([own_up[i], zero], axis=1)], axis=0)
            ghost_a[i] = jnp.concatenate([jnp.concatenate([from_below[i], zero], axis=1),
                                          jnp.concatenate([zero, from_above[i]], axis=1)], axis=0)
            cross_a[i] = jnp.concatenate([jnp.concatenate([up[i], zero], axis=1),
                                          jnp.concatenate([zero, down[i]], axis=1)], axis=0)

    def pair_of(refs, i, low, high):
        p = 2 * i
        return [jnp.concatenate([
            jnp.concatenate([ref[p + j, BLK * low:BLK * (low + 1), :], ref[p + j, BLK * high:BLK * (high + 1), :]], axis=0)
            for j in range(2)], axis=1) for ref in refs]

    def add_ghosts(inverses):
        def one(i, carry):
            for j in range(2):
                p = 2 * i + j
                for side, row in ((0, 0), (1, 3)):
                    high, low = halves(ghost[side, pl.ds(p, BLK, stride=PHYS), :] * inverses)
                    xh[p, BLK * row:BLK * (row + 1), :] = high
                    xl[p, BLK * row:BLK * (row + 1), :] = low
            value = (split_dot((ghost_a[0], ghost_a[1]), pair_of((xh, xl), i, 0, 3))
                     + split_dot((own_a[0], own_a[1]), pair_of((xh, xl), i, 1, 2)))
            for k in range(2):
                for j in range(2):
                    both = w0[k, 2 * i + j] + value[BLK * k:BLK * (k + 1), BLK * j:BLK * (j + 1)]
                    w0[k, 2 * i + j] = both
                    partial[k, 2 * i + j] = both
            return carry

        lax.fori_loop(0, PAIRS, one, 0)

    def base_down():
        return remote(partial.at[0], w_ghost.at[1], send_w.at[0], recv_w.at[0], below)

    def base_up():
        return remote(partial.at[1], w_ghost.at[0], send_w.at[1], recv_w.at[1], above)

    send(0, 1, yw)
    send(0, 0, qw)
    send_far(0)
    q012 = product(q2, q01)
    y012 = carry_over(q2, y01, s2)
    inverses = start_wave()
    make_phys()
    yw = carry_over(qw, receive(0, 1), yw)
    send(1, 1, yw)
    send_far(1)
    qw = product(qw, receive(0, 0))
    send(1, 0, qw)
    phys_product(xh, xl, w0)

    @pl.when(has_below)
    def _():
        coupling_up().wait_recv()
        ghost_up().wait_recv()

    @pl.when(has_above)
    def _():
        ghost_down().wait_recv()

    make_ghost_matrices()
    add_ghosts(inverses)

    @pl.when(has_below)
    def _():
        base_down().start()

    @pl.when(has_above)
    def _():
        base_up().start()

    yw = carry_over(qw, receive(1, 1), yw)
    send(2, 1, yw)
    send_far(2)
    send(2, 0, product(qw, receive(1, 0)))

    @pl.when(zz >= 5)
    def _():
        remote(window.at[2, 1], far, send_f.at[0], recv_f.at[0], in_column(zz - 5)).wait_recv()
    y_near = receive(2, 1)
    start = carry_over(receive(2, 0), far[...], y_near)

    def owner(slot):
        return slot + odd * (NX - 1 - 2 * slot)

    def give(slot):
        return remote(ends.at[slot], envs.at[x], send_e.at[slot], recv_e.at[x], in_row(owner(slot)))

    ends[0] = start
    for slot, (q, y) in enumerate(((q0, s0), (q01, y01), (q012, y012))):
        ends[slot + 1] = carry_over(q, start, y)
    for hop in (2, 1, 3):
        for slot in range(NX):
            @pl.when(slot == lax.rem(my_slot + hop, NX))
            def _():
                give(slot).start()
    envs[pl.ds(x, 1)] = ends[pl.ds(my_slot, 1)]
    for column in range(NX):
        @pl.when(x != column)
        def _():
            remote(ends.at[column], envs.at[column], send_e.at[column], recv_e.at[column], in_row(column)).wait_recv()

    def envs_down():
        return remote(envs.at[pl.ds(0, 2)], lr_ghost.at[1], send_v.at[3], recv_v.at[3], below)

    def envs_up():
        return remote(envs.at[pl.ds(2, 2)], lr_ghost.at[0], send_v.at[4], recv_v.at[4], above)

    @pl.when(has_below)
    def _():
        envs_down().start()

    @pl.when(has_above)
    def _():
        envs_up().start()

    def right_of(env):
        high, low = halves(env)
        return jnp.concatenate([jnp.concatenate([high, low], axis=1),
                                jnp.concatenate([high, jnp.zeros_like(low)], axis=1)], axis=0)

    for k in range(2):
        left_ref[k] = envs[2 * k]
        right_w[k] = right_of(envs[2 * k + 1])
    none = jnp.zeros((BLK, BLK), BF16)
    lefts = [halves(envs[2 * k]) for k in range(2)]
    for h in range(2):
        own_l[h] = jnp.concatenate([jnp.concatenate([lefts[0][h], none], axis=1),
                                    jnp.concatenate([none, lefts[1][h]], axis=1)], axis=0)
        own_a[h] = own_a[h] + own_l[h]

    def product_of(refs, i, low, high, left, rights):
        p = 2 * i
        value = split_dot((left[0], left[1]), pair_of(refs, i, low, high))
        blocks = []
        for k, row in enumerate((low, high)):
            rows = slice(BLK * row, BLK * (row + 1))
            lhs = jnp.concatenate([jnp.concatenate([ref[p + j, rows, :] for ref in refs], axis=1)
                                   for j in range(2)], axis=0)
            right = dot(lhs, right_w[rights + k])
            right = right[:, :BLK] + right[:, BLK:]
            blocks.append([value[BLK * k:BLK * (k + 1), BLK * j:BLK * (j + 1)] + right[BLK * j:BLK * (j + 1)]
                           for j in range(2)])
        return blocks

    def first_apply(i, total):
        blocks = product_of((xh, xl), i, 1, 2, own_l, 0)
        for k in range(2):
            for j in range(2):
                p = 2 * i + j
                value = w0[k, p] + blocks[k][j]
                w0[k, p] = value
                high, low = halves(value)
                yh[p, BLK * (k + 1):BLK * (k + 2), :] = high
                yl[p, BLK * (k + 1):BLK * (k + 2), :] = low
                total = total + fold(value * vp[k, p])
        return total

    def ghost_apply(i, carry):
        blocks = product_of((xh, xl), i, 0, 3, ghost_l, 2)
        for side, row in ((0, 0), (1, 3)):
            for j in range(2):
                p = 2 * i + j
                high, low = halves(w_ghost[side, p] + blocks[side][j])
                yh[p, BLK * row:BLK * (row + 1), :] = high
                yl[p, BLK * row:BLK * (row + 1), :] = low
        return carry

    zeros = jnp.zeros((8, BLK), F32)
    spread(1, [lax.fori_loop(0, PAIRS, first_apply, zeros)])
    phys_product(yh, yl, w1)

    @pl.when(has_below)
    def _():
        base_up().wait_recv()
        envs_up().wait_recv()

    @pl.when(has_above)
    def _():
        base_down().wait_recv()
        envs_down().wait_recv()

    lefts = [halves(lr_ghost[side, 0]) for side in range(2)]
    for h in range(2):
        ghost_l[h] = jnp.concatenate([jnp.concatenate([lefts[0][h], none], axis=1),
                                      jnp.concatenate([none, lefts[1][h]], axis=1)], axis=0)
    for side in range(2):
        right_w[2 + side] = right_of(lr_ghost[side, 1])
    lax.fori_loop(0, PAIRS, ghost_apply, 0)
    corr = collect(1, 1)[0]
    corrs = jnp.broadcast_to(corr, (BLK, BLK))

    def finish(i, totals):
        rr, w0r, rt, vt, w0t, tt = totals
        blocks = product_of((yh, yl), i, 1, 2, own_a, 0)
        value = split_dot((ghost_a[0], ghost_a[1]), pair_of((yh, yl), i, 0, 3))
        for k in range(2):
            for j in range(2):
                p = 2 * i + j
                applied = w0[k, p]
                wave = vp[k, p]
                residual = applied - corrs * wave
                turned = (w1[k, p] + blocks[k][j] + value[BLK * k:BLK * (k + 1), BLK * j:BLK * (j + 1)]
                          - corrs * applied)
                r0[k, p] = residual
                w1[k, p] = turned
                high, low = halves(turned)
                xh[p, BLK * (k + 1):BLK * (k + 2), :] = high
                xl[p, BLK * (k + 1):BLK * (k + 2), :] = low
                rr = rr + fold(residual * residual)
                w0r = w0r + fold(applied * residual)
                rt = rt + fold(residual * turned)
                vt = vt + fold(wave * turned)
                w0t = w0t + fold(applied * turned)
                tt = tt + fold(turned * turned)
        return rr, w0r, rt, vt, w0t, tt

    def turned_down(part):
        at = pl.ds(2 * part, 2)
        return remote(w1.at[0, at], t_ghost.at[0, at], send_t.at[0, part], recv_t.at[0, part], below)

    def turned_up(part):
        return remote(w1.at[1, pl.ds(PAIRS + 2 * part, 2)], t_ghost.at[1, pl.ds(2 * part, 2)],
                      send_t.at[1, part], recv_t.at[1, part], above)

    totals = (zeros,) * 6
    for part in range(CHUNKS):
        totals = lax.fori_loop(0, 2, lambda n, c: finish(part + CHUNKS * n, c), totals)

        @pl.when(has_below)
        def _():
            turned_down(part).start()

        @pl.when(has_above)
        def _():
            turned_up(part).start()
    w0t, tt = totals[4:]
    spread(2, list(totals[:4]))

    def third_apply(i, total):
        blocks = product_of((xh, xl), i, 1, 2, own_a, 0)
        for k in range(2):
            for j in range(2):
                total = total + fold(blocks[k][j] * w1[k, 2 * i + j])
        return total

    def third_phys(i, total):
        for k in range(2):
            value = phys_piece(xh, xl, k, i)
            at = pl.multiple_of(32 * i, 32)
            for p in range(PHYS):
                rows = value[PHYS * p:PHYS * (p + 1)]
                both = jnp.concatenate([rows[:, :BLK], rows[:, BLK:]], axis=0)
                total = total + fold(both * w1[k, p, pl.ds(at, 32), :])
        return total

    def cross(i, carry):
        p = 2 * i
        rhs = [jnp.concatenate([
            jnp.concatenate([ref[p + j, 2 * BLK:3 * BLK, :], ref[p + PAIRS + j, BLK:2 * BLK, :]], axis=0)
            for j in range(2)], axis=1) for ref in (xh, xl)]
        value = split_dot((cross_a[0], cross_a[1]), rhs)
        for side in range(2):
            for j in range(2):
                crossed[side, p + j] = value[BLK * side:BLK * (side + 1), BLK * j:BLK * (j + 1)]
        return carry

    lax.fori_loop(0, PAIRS // 2, cross, 0)
    tht = lax.fori_loop(0, PAIRS, third_apply, zeros)
    tht = lax.fori_loop(0, BLK // 32, third_phys, tht)

    rr, w0r, rt, vt = collect(2, 4)
    norm = jnp.sqrt(rr + EPS)
    curvature = rt / (rr + EPS)
    coupled = w0r / norm
    ritz = 0.5 * (corr + curvature) - jnp.sqrt(0.25 * (corr - curvature) ** 2 + coupled * coupled)
    coef = ritz - corr
    magnitude = jnp.sqrt(coupled * coupled + coef * coef)
    wave_v = coupled / magnitude
    wave_r = coef / (magnitude * norm)
    corr2 = wave_v * wave_v * corr + wave_v * wave_r * (vt + w0r) + wave_r * wave_r * rt
    res_v = wave_v * (corr - corr2)
    res_r = wave_v - corr2 * wave_r
    res_t = wave_r

    loads[5].wait()
    masks = [(lax.broadcasted_iota(jnp.int32, (1, BLK), 1) < kept_ref[0, k]).astype(F32) for k in range(2)]
    wide = [jnp.broadcast_to(value, (BLK, BLK)) for value in (wave_v, wave_r, wave_v * corr, res_v, res_r, res_t)]

    def second_residual(p, totals):
        rr2, ar2, mww, mwr, mrr = totals
        for k in range(2):
            wave, residual, turned = vp[k, p], r0[k, p], w1[k, p]
            now = wide[0] * wave + wide[1] * residual
            applied = wide[2] * wave + wide[0] * residual + wide[1] * turned
            second = wide[3] * wave + wide[4] * residual + wide[5] * turned
            rr2 = rr2 + fold(second * second)
            ar2 = ar2 + fold(applied * second)
            mww = mww + masks[k] * fold(now * now)
            mwr = mwr + masks[k] * fold(now * second)
            mrr = mrr + masks[k] * fold(second * second)
        return rr2, ar2, mww, mwr, mrr

    finals = lax.fori_loop(0, PHYS, second_residual, (zeros,) * 5)

    for part in range(CHUNKS):
        @pl.when(has_above)
        def _():
            turned_down(part).wait_recv()

        @pl.when(has_below)
        def _():
            turned_up(part).wait_recv()

    def meet(i, total):
        return total + fold(crossed[0, i] * t_ghost[0, i]) + fold(crossed[1, i] * t_ghost[1, i])

    tht = tht + 2.0 * lax.fori_loop(0, PAIRS, meet, zeros)
    spread(3, list(finals) + [tht, w0t, tt])
    rr2, ar2, mww, mwr, mrr, tht, w0t, tt = collect(3, 8)
    norm2 = jnp.sqrt(rr2 + EPS)
    turned2 = (res_v * res_v * corr + res_r * res_r * rt + res_t * res_t * tht
               + 2.0 * (res_v * res_r * vt + res_v * res_t * w0t + res_r * res_t * tt))
    curvature = turned2 / (rr2 + EPS)
    coupled = ar2 / norm2
    ritz = 0.5 * (corr2 + curvature) - jnp.sqrt(0.25 * (corr2 - curvature) ** 2 + coupled * coupled)
    coef = ritz - corr2
    magnitude = jnp.sqrt(coupled * coupled + coef * coef)
    of_wave = coupled / magnitude
    of_res = coef / (magnitude * norm2)
    kept = of_wave * of_wave * mww + 2.0 * of_wave * of_res * mwr + of_res * of_res * mrr
    scale = 1.0 / jnp.sqrt(kept + EPS)
    energy_ref[...] = jnp.broadcast_to(ritz, (8, BLK))
    last = [jnp.broadcast_to(scale * value, (BLK, BLK)) for value in (
        of_wave * wave_v + of_res * res_v, of_wave * wave_r + of_res * res_r, of_res * res_t)]

    def write(p, carry):
        for k in range(2):
            value = last[0] * vp[k, p] + last[1] * r0[k, p] + last[2] * w1[k, p]
            out_ref[k, p] = value * masks[k]
        return carry

    lax.fori_loop(0, PHYS, write, 0)

    for column in range(NX):
        @pl.when(x != column)
        def _():
            deal(column).wait_send()
    for at in range(3):
        for part in range(2):
            @pl.when(sends[at][part])
            def _():
                step(at, part).wait_send()

    @pl.when(zz < 3)
    def _():
        far_copy(0).wait_send()
    for slot in range(NX):
        @pl.when(my_slot != slot)
        def _():
            give(slot).wait_send()
    for at in range(4):
        for hop in range(1, NS):
            remote(sums.at[at, sector], sums.at[at, sector], send_p.at[at, hop], recv_p.at[at, sector],
                   (chain, peer(hop))).wait_send()

    @pl.when(has_above)
    def _():
        coupling_up().wait_send()
        ghost_up().wait_send()
        base_up().wait_send()
        envs_up().wait_send()
        for part in range(CHUNKS):
            turned_up(part).wait_send()

    @pl.when(has_below)
    def _():
        ghost_down().wait_send()
        base_down().wait_send()
        envs_down().wait_send()
        for part in range(CHUNKS):
            turned_down(part).wait_send()


def write_kernel(wave_ref, energy_in, left_in, out_ref, energy_ref, left_ref, rows, sem):
    left_copy = pltpu.make_async_copy(left_in, left_ref, sem.at[8])
    left_copy.start()
    energy_ref[0] = jnp.sum(energy_in[0:1, 0:1])
    copies = []
    for k in range(2):
        for part in range(CHUNKS):
            size = ROWS // CHUNKS
            for p in range(PHYS):
                rows[k, pl.ds(size * part + p, size // PHYS, stride=PHYS), :] = (
                    wave_ref[k, p, size // PHYS * part:size // PHYS * (part + 1), :])
            at = pl.ds(size * part, size)
            copies.append(pltpu.make_async_copy(rows.at[k, at], out_ref.at[k, at], sem.at[CHUNKS * k + part]))
            copies[-1].start()
    for copy in copies:
        copy.wait()
    left_copy.wait()


def per_device(wave_start, transfer, energy_terms, coupling, physical, kept_ranks):
    hbm = pl.BlockSpec(memory_space=pltpu.HBM)
    vmem = pl.BlockSpec(memory_space=pltpu.VMEM)
    smem = pl.BlockSpec(memory_space=pltpu.SMEM)
    dma = pltpu.SemaphoreType.DMA

    def square(*lead):
        return pltpu.VMEM((*lead, BLK, BLK), F32)

    def wide(*lead):
        return pltpu.VMEM((*lead, 2 * BLK, 2 * BLK), BF16)

    split_waves = pltpu.VMEM((PHYS, 4 * BLK, BLK), BF16)
    wave, energy, left = pl.pallas_call(
        update_kernel,
        out_shape=(
            jax.ShapeDtypeStruct((2, PHYS, BLK, BLK), F32),
            jax.ShapeDtypeStruct((8, BLK), F32),
            jax.ShapeDtypeStruct((2, BLK, BLK), F32),
        ),
        in_specs=[hbm] * 6,
        out_specs=(vmem, vmem, vmem),
        scratch_shapes=[
            pltpu.VMEM((2, ROWS, BLK), F32), square(2), square(2), square(2), pltpu.VMEM((PHYS, PHYS), F32),
            pltpu.SMEM((1, 2), jnp.int32),
            square(NX, 2), square(NX, 2), square(3, 2), square(3, 2), square(), square(2, PHYS), square(NX), square(NX),
            pltpu.VMEM((2, ROWS, BLK), F32), square(), square(2, PHYS), square(2, PHYS), square(2, PHYS), square(2, PHYS),
            square(2, PHYS), square(2, PAIRS), square(2, 2), square(2, PAIRS),
            split_waves, split_waves, split_waves, split_waves,
            wide(2), wide(2), wide(2), wide(2), wide(2), wide(4), wide(2),
            pltpu.VMEM((4, NS, 8, BLK), F32),
            dma((6,)), dma((NX,)), dma((NX,)), dma((3, 2)), dma((3, 2)), dma((1,)), dma((1,)), dma((NX,)), dma((NX,)),
            dma((5,)), dma((5,)), dma((2,)), dma((2,)), dma((2, CHUNKS)), dma((2, CHUNKS)),
            dma((4, NS)), dma((4, NS)),
        ],
        compiler_params=pltpu.CompilerParams(
            collective_id=0, has_side_effects=True, vmem_limit_bytes=50 << 20),
    )(*[pltpu.with_memory_space_constraint(value, pltpu.HBM) for value in (
        wave_start.reshape(2, ROWS, BLK), transfer[0], energy_terms[0], coupling[0], physical[0], kept_ranks)])
    out, energy, left = pl.pallas_call(
        write_kernel,
        out_shape=(
            jax.ShapeDtypeStruct((2, ROWS, BLK), F32),
            jax.ShapeDtypeStruct((1,), F32),
            jax.ShapeDtypeStruct((2, BLK, BLK), F32),
        ),
        in_specs=[vmem] * 3,
        out_specs=(hbm, smem, hbm),
        scratch_shapes=[pltpu.VMEM((2, ROWS, BLK), F32), dma((9,))],
    )(*[pltpu.with_memory_space_constraint(value, pltpu.VMEM) for value in (wave, energy, left)])
    return (out.reshape(wave_start.shape), energy, left[None])


def solution(mesh):
    placed = (
        P("chain", "sector", None, None, None),
        P("chain", "sector", None, None),
        P("chain", "sector", None, None),
        P("chain", "sector", None, None),
        P("chain", None, None),
        P("chain", "sector"),
    )
    return jax.shard_map(
        per_device,
        mesh=mesh,
        in_specs=placed,
        out_specs=(
            P("chain", "sector", None, None, None),
            P("chain"),
            P("chain", "sector", None, None),
        ),
        check_vma=False,
    )
```

time: 88.8 us -> 71 us (0.80)
  Pallas kernels: 79.6 us -> 70.2 us
  local copies, waits for them, and re-layouts: 8.27 us -> 0 us
    pallas_call x1 -> x2, Pallas kernels: 79.6 us -> 70.2 us  [the longest x1 68 us: per_device(): pl.pallas_call(update_kernel, out_shape=(jax.ShapeDtypeStruct((2, PHYS, B...]
    unnamed x12 -> x0, local copies, waits for them, and re-layouts: 7.75 us -> none
where the time goes in v3:
time: 71 us; the launch traced here: 70.9 us
  Pallas kernels  70.2 us (99%)
    pallas_call x1, Pallas kernels, per_device(): pl.pallas_call(update_kernel, out_shape=(jax.ShapeDtypeStruct((2, PHYS, B...  68 us
    pallas_call x1, Pallas kernels, per_device(): pl.pallas_call(write_kernel, out_shape=(jax.ShapeDtypeStruct((2, ROWS, BL...  2.2 us

profile of v3, /device:TPU:1, one launch (start us, length us, event | category | flops | bytes accessed | tf_op | source)
XLA Modules:
  0.0 70.9 jit_solution(13124915401279489574)
XLA Ops:
  0.6 68.0 %shard_map.85 = (f32[2,16,128,128]{3,2,1,0:T(8,128)S(1)}, f32[8,128]{1,0:T(8,128)S(1)}, f32[2,128,128]{2,1,0:T(8,128)S(1)}) custom-call(f32[2,2048,128]{2,1,0:T(8,128)} %bitcast.7, f32[2,128,128]{2,1,0:T(8,128)} %bitcast.8, f32[2,128,128]{2,1,0:T(8,128)} %bitcast.9, f32[2,128,128]{2,1,0:T(8,128)} %bitcast.10, f32[16,16]{1,0:T(8,128)} %bitcast.11, ...), custom_call_target="tpu_custom_call" | custom-call | tf_op jit(solution)/shard_map/pallas_call | solution.py:722
  68.7 2.2 %shard_map.86 = (f32[2,2048,128]{2,1,0:T(8,128)}, f32[1]{0:T(128)}, f32[2,128,128]{2,1,0:T(8,128)}) custom-call(f32[2,16,128,128]{3,2,1,0:T(8,128)S(1)} %get-tuple-element.9.wave_ref, f32[8,128]{1,0:T(8,128)S(1)} %get-tuple-element.10.energy_in, f32[2,128,128]{2,1,0:T(8,128)S(1)} %get-tuple-element.11.left_in), custom_call_target="tpu_custom_call" | custom-call | tf_op jit(solution)/shard_map/pallas_call | solution.py:748

commit v4 on v3

--- a/solution.py
+++ b/solution.py
@@ -46,6 +46,20 @@
     return dot(lhs[0], rhs[0]) + (dot(lhs[0], rhs[1]) + dot(lhs[1], rhs[0]))
 
 
+def packed(matrix):
+    high, low = halves(matrix)
+    return jnp.concatenate([jnp.concatenate([high, high], axis=1),
+                            jnp.concatenate([low, jnp.zeros_like(low)], axis=1)], axis=0)
+
+
+def packed_dot(matrix, refs, p, row):
+    rows = slice(BLK * row, BLK * (row + 1))
+    rhs = jnp.concatenate([jnp.concatenate([ref[p + j, rows, :] for ref in refs], axis=0) for j in range(2)], axis=1)
+    value = dot(matrix, rhs)
+    value = value[:BLK] + value[BLK:]
+    return value[:, :BLK], value[:, BLK:]
+
+
 def carry_over(matrix, env, source):
     return product(product(matrix, env), matrix, NT) + source
 
@@ -58,11 +72,11 @@
     return pltpu.make_async_remote_copy(src, dst, send_sem, recv_sem, device_id=device, device_id_type=MESH)
 
 
-def update_kernel(v_hbm, t_hbm, e_hbm, c_hbm, p_hbm, kept_hbm, out_ref, energy_ref, left_ref,
+def update_kernel(v_hbm, t_hbm, e_hbm, c_hbm, p_hbm, kept_hbm, vp, r0, w1, last_ref, left_ref,
                   v_ref, t_ref, e_ref, c_ref, p_ref, kept_ref,
-                  mine, elements, window, came, far, partial, ends, envs,
-                  ghost, ghost_c, vp, w0, r0, w1, w_ghost, t_ghost, lr_ghost, crossed,
-                  xh, xl, yh, yl, own_l, own_a, ghost_a, cross_a, ghost_l, right_w, phys_a, sums,
+                  mine, elements, window, came, far, partial, outward, ends, envs,
+                  ghost, ghost_c, w0, w_ghost, t_ghost, lr_ghost, crossed,
+                  xh, xl, yh, yl, left_w, own_a, ghost_a, cross_a, right_w, phys_a, sums,
                   load, send_a, recv_a, send_z, recv_z, send_f, recv_f, send_e, recv_e,
                   send_v, recv_v, send_w, recv_w, send_t, recv_t, send_p, recv_p):
     chain = lax.axis_index("chain")
@@ -121,7 +135,7 @@
 
     def spread(at, parts):
         rows = [jnp.sum(part, axis=0, keepdims=True) for part in parts]
-        rows += [jnp.zeros((1, BLK), F32)] * (8 - len(rows))
+        rows += [jnp.zeros((1, BLK), F32)] * (16 - len(rows))
         sums[at, pl.ds(sector, 1)] = jnp.concatenate(rows, axis=0)[None]
         for hop in range(1, NS):
             remote(sums.at[at, sector], sums.at[at, sector], send_p.at[at, hop], recv_p.at[at, sector],
@@ -161,11 +175,6 @@
     @pl.when(has_above)
     def _():
         coupling_up().start()
-        ghost_up().start()
-
-    @pl.when(has_below)
-    def _():
-        ghost_down().start()
 
     def square(i, total):
         part = v_ref[:, pl.ds(pl.multiple_of(i * 256, 256), 256), :]
@@ -188,14 +197,14 @@
         ghost[0] = jnp.zeros((ROWS, BLK), F32)
         ghost_c[...] = square_zero
         w_ghost[0] = jnp.zeros((PHYS, BLK, BLK), F32)
-        t_ghost[1] = jnp.zeros((PAIRS, BLK, BLK), F32)
+        t_ghost[0] = jnp.zeros((PAIRS, BLK, BLK), F32)
         lr_ghost[0] = jnp.zeros((2, BLK, BLK), F32)
 
     @pl.when(sector == NS - 1)
     def _():
         ghost[1] = jnp.zeros((ROWS, BLK), F32)
         w_ghost[1] = jnp.zeros((PHYS, BLK, BLK), F32)
-        t_ghost[0] = jnp.zeros((PAIRS, BLK, BLK), F32)
+        t_ghost[1] = jnp.zeros((PAIRS, BLK, BLK), F32)
         lr_ghost[1] = jnp.zeros((2, BLK, BLK), F32)
 
     for slot in range(NX):
@@ -203,6 +212,14 @@
         def _():
             remote(mine.at[slot], elements.at[slot], send_a.at[slot], recv_a.at[slot],
                    in_row(lax.rem(x + 1, NX))).wait_recv()
+
+    @pl.when(has_above)
+    def _():
+        ghost_up().start()
+
+    @pl.when(has_below)
+    def _():
+        ghost_down().start()
 
     q0, q1, q2, q3 = [elements[s, 0] for s in range(NX)]
     s0, s1, s2, s3 = [elements[s, 1] for s in range(NX)]
@@ -272,13 +289,15 @@
             for p in range(PHYS):
                 phys_a[i, PHYS * p:PHYS * (p + 1), :] = (wide[p:p + 1, :] * same).astype(BF16)
 
-    def phys_piece(high, low, k, i):
+    def phys_rows(ref, k, i):
         first = pl.multiple_of(BLK * (k + 1) + 32 * i, 32)
         second = pl.multiple_of(BLK * (k + 1) + 32 * i + 16, 16)
-        rhs = [jnp.concatenate([
+        return jnp.concatenate([
             jnp.concatenate([ref[p, pl.ds(at, 16), :] for p in range(PHYS)], axis=0)
-            for at in (first, second)], axis=1) for ref in (high, low)]
-        return split_dot((phys_a[0], phys_a[1]), rhs)
+            for at in (first, second)], axis=1)
+
+    def phys_piece(high, low, k, i):
+        return split_dot((phys_a[0], phys_a[1]), (phys_rows(high, k, i), phys_rows(low, k, i)))
 
     def phys_product(high, low, dst):
         def one(i, carry):
@@ -295,19 +314,16 @@
     def make_ghost_matrices():
         loads[3].wait()
         zero = jnp.zeros((BLK, BLK), BF16)
-        from_below = halves(ghost_c[...])
-        from_above = halves(c_ref[1].T)
-        up = halves(c_ref[1])
-        down = halves(ghost_c[...].T)
         own_up = halves(c_ref[0])
         own_down = halves(c_ref[0].T)
         for i in range(2):
             own_a[i] = jnp.concatenate([jnp.concatenate([zero, own_down[i]], axis=1),
                                         jnp.concatenate([own_up[i], zero], axis=1)], axis=0)
-            ghost_a[i] = jnp.concatenate([jnp.concatenate([from_below[i], zero], axis=1),
-                                          jnp.concatenate([zero, from_above[i]], axis=1)], axis=0)
-            cross_a[i] = jnp.concatenate([jnp.concatenate([up[i], zero], axis=1),
-                                          jnp.concatenate([zero, down[i]], axis=1)], axis=0)
+        last = c_ref[1] * has_above.astype(F32)
+        ghost_a[0] = packed(ghost_c[...])
+        ghost_a[1] = packed(last.T)
+        cross_a[0] = packed(ghost_c[...].T)
+        cross_a[1] = packed(last)
 
     def pair_of(refs, i, low, high):
         p = 2 * i
@@ -315,24 +331,34 @@
             jnp.concatenate([ref[p + j, BLK * low:BLK * (low + 1), :], ref[p + j, BLK * high:BLK * (high + 1), :]], axis=0)
             for j in range(2)], axis=1) for ref in refs]
 
-    def add_ghosts(inverses):
-        def one(i, carry):
+    def add_own(i, carry):
+        value = split_dot((own_a[0], own_a[1]), pair_of((xh, xl), i, 1, 2))
+        for k in range(2):
             for j in range(2):
                 p = 2 * i + j
-                for side, row in ((0, 0), (1, 3)):
-                    high, low = halves(ghost[side, pl.ds(p, BLK, stride=PHYS), :] * inverses)
-                    xh[p, BLK * row:BLK * (row + 1), :] = high
-                    xl[p, BLK * row:BLK * (row + 1), :] = low
-            value = (split_dot((ghost_a[0], ghost_a[1]), pair_of((xh, xl), i, 0, 3))
-                     + split_dot((own_a[0], own_a[1]), pair_of((xh, xl), i, 1, 2)))
-            for k in range(2):
-                for j in range(2):
-                    both = w0[k, 2 * i + j] + value[BLK * k:BLK * (k + 1), BLK * j:BLK * (j + 1)]
-                    w0[k, 2 * i + j] = both
-                    partial[k, 2 * i + j] = both
-            return carry
-
-        lax.fori_loop(0, PAIRS, one, 0)
+                both = w0[k, p] + value[BLK * k:BLK * (k + 1), BLK * j:BLK * (j + 1)]
+                w0[k, p] = both
+                partial[k, p] = both
+        return carry
+
+    def add_to_ghosts(i, carry):
+        for side in range(2):
+            blocks = packed_dot(cross_a[side], (xh, xl), 2 * i, side + 1)
+            for j in range(2):
+                outward[side, 2 * i + j] = blocks[j]
+        return carry
+
+    def add_ghosts(i, inverses):
+        for side, row in ((0, 0), (1, 3)):
+            for j in range(2):
+                p = 2 * i + j
+                high, low = halves(ghost[side, pl.ds(p, BLK, stride=PHYS), :] * inverses)
+                xh[p, BLK * row:BLK * (row + 1), :] = high
+                xl[p, BLK * row:BLK * (row + 1), :] = low
+            blocks = packed_dot(ghost_a[side], (xh, xl), 2 * i, row)
+            for j in range(2):
+                w0[side, 2 * i + j] = w0[side, 2 * i + j] + blocks[j]
+        return inverses
 
     def base_down():
         return remote(partial.at[0], w_ghost.at[1], send_w.at[0], recv_w.at[0], below)
@@ -347,24 +373,19 @@
     y012 = carry_over(q2, y01, s2)
     inverses = start_wave()
     make_phys()
+
+    @pl.when(has_below)
+    def _():
+        coupling_up().wait_recv()
+
+    make_ghost_matrices()
     yw = carry_over(qw, receive(0, 1), yw)
     send(1, 1, yw)
     send_far(1)
     qw = product(qw, receive(0, 0))
     send(1, 0, qw)
     phys_product(xh, xl, w0)
-
-    @pl.when(has_below)
-    def _():
-        coupling_up().wait_recv()
-        ghost_up().wait_recv()
-
-    @pl.when(has_above)
-    def _():
-        ghost_down().wait_recv()
-
-    make_ghost_matrices()
-    add_ghosts(inverses)
+    lax.fori_loop(0, PAIRS, add_own, 0)
 
     @pl.when(has_below)
     def _():
@@ -378,6 +399,16 @@
     send(2, 1, yw)
     send_far(2)
     send(2, 0, product(qw, receive(1, 0)))
+
+    @pl.when(has_below)
+    def _():
+        ghost_up().wait_recv()
+
+    @pl.when(has_above)
+    def _():
+        ghost_down().wait_recv()
+
+    inverses = lax.fori_loop(0, PAIRS // 2, add_ghosts, inverses)
 
     @pl.when(zz >= 5)
     def _():
@@ -400,6 +431,8 @@
             def _():
                 give(slot).start()
     envs[pl.ds(x, 1)] = ends[pl.ds(my_slot, 1)]
+    lax.fori_loop(PAIRS // 2, PAIRS, add_ghosts, inverses)
+    lax.fori_loop(0, PAIRS, add_to_ghosts, 0)
     for column in range(NX):
         @pl.when(x != column)
         def _():
@@ -428,32 +461,32 @@
         left_ref[k] = envs[2 * k]
         right_w[k] = right_of(envs[2 * k + 1])
     none = jnp.zeros((BLK, BLK), BF16)
+
     lefts = [halves(envs[2 * k]) for k in range(2)]
     for h in range(2):
-        own_l[h] = jnp.concatenate([jnp.concatenate([lefts[0][h], none], axis=1),
-                                    jnp.concatenate([none, lefts[1][h]], axis=1)], axis=0)
-        own_a[h] = own_a[h] + own_l[h]
-
-    def product_of(refs, i, low, high, left, rights):
-        p = 2 * i
-        value = split_dot((left[0], left[1]), pair_of(refs, i, low, high))
-        blocks = []
-        for k, row in enumerate((low, high)):
-            rows = slice(BLK * row, BLK * (row + 1))
-            lhs = jnp.concatenate([jnp.concatenate([ref[p + j, rows, :] for ref in refs], axis=1)
-                                   for j in range(2)], axis=0)
-            right = dot(lhs, right_w[rights + k])
-            right = right[:, :BLK] + right[:, BLK:]
-            blocks.append([value[BLK * k:BLK * (k + 1), BLK * j:BLK * (j + 1)] + right[BLK * j:BLK * (j + 1)]
-                           for j in range(2)])
-        return blocks
+        own_a[h] = own_a[h] + jnp.concatenate([jnp.concatenate([lefts[0][h], none], axis=1),
+                                               jnp.concatenate([none, lefts[1][h]], axis=1)], axis=0)
+        left_w[h] = packed(envs[2 * h])
+
+    def right_products(refs, p, row, matrix):
+        rows = slice(BLK * row, BLK * (row + 1))
+        lhs = jnp.concatenate([jnp.concatenate([ref[p + j, rows, :] for ref in refs], axis=1)
+                               for j in range(2)], axis=0)
+        value = dot(lhs, matrix)
+        value = value[:, :BLK] + value[:, BLK:]
+        return value[:BLK], value[BLK:]
+
+    def environment_products(refs, i, row, at):
+        lefts = packed_dot(left_w[at], refs, 2 * i, row)
+        rights = right_products(refs, 2 * i, row, right_w[at])
+        return [left + right for left, right in zip(lefts, rights)]
 
     def first_apply(i, total):
-        blocks = product_of((xh, xl), i, 1, 2, own_l, 0)
         for k in range(2):
+            blocks = environment_products((xh, xl), i, k + 1, k)
             for j in range(2):
                 p = 2 * i + j
-                value = w0[k, p] + blocks[k][j]
+                value = w0[k, p] + blocks[j]
                 w0[k, p] = value
                 high, low = halves(value)
                 yh[p, BLK * (k + 1):BLK * (k + 2), :] = high
@@ -462,11 +495,11 @@
         return total
 
     def ghost_apply(i, carry):
-        blocks = product_of((xh, xl), i, 0, 3, ghost_l, 2)
         for side, row in ((0, 0), (1, 3)):
+            blocks = environment_products((xh, xl), i, row, 2 + side)
             for j in range(2):
                 p = 2 * i + j
-                high, low = halves(w_ghost[side, p] + blocks[side][j])
+                high, low = halves(w_ghost[side, p] + outward[side, p] + blocks[j])
                 yh[p, BLK * row:BLK * (row + 1), :] = high
                 yl[p, BLK * row:BLK * (row + 1), :] = low
         return carry
@@ -477,35 +510,40 @@
 
     @pl.when(has_below)
     def _():
+        envs_up().wait_recv()
+
+    @pl.when(has_above)
+    def _():
+        envs_down().wait_recv()
+
+    for side in range(2):
+        left_w[2 + side] = packed(lr_ghost[side, 0])
+        right_w[2 + side] = right_of(lr_ghost[side, 1])
+
+    @pl.when(has_below)
+    def _():
         base_up().wait_recv()
-        envs_up().wait_recv()
 
     @pl.when(has_above)
     def _():
         base_down().wait_recv()
-        envs_down().wait_recv()
-
-    lefts = [halves(lr_ghost[side, 0]) for side in range(2)]
-    for h in range(2):
-        ghost_l[h] = jnp.concatenate([jnp.concatenate([lefts[0][h], none], axis=1),
-                                      jnp.concatenate([none, lefts[1][h]], axis=1)], axis=0)
-    for side in range(2):
-        right_w[2 + side] = right_of(lr_ghost[side, 1])
+
     lax.fori_loop(0, PAIRS, ghost_apply, 0)
     corr = collect(1, 1)[0]
     corrs = jnp.broadcast_to(corr, (BLK, BLK))
 
     def finish(i, totals):
-        rr, w0r, rt, vt, w0t, tt = totals
-        blocks = product_of((yh, yl), i, 1, 2, own_a, 0)
-        value = split_dot((ghost_a[0], ghost_a[1]), pair_of((yh, yl), i, 0, 3))
+        rr, rt, vt, tt = totals
+        value = split_dot((own_a[0], own_a[1]), pair_of((yh, yl), i, 1, 2))
         for k in range(2):
+            ghosts = packed_dot(ghost_a[k], (yh, yl), 2 * i, 3 * k)
+            rights = right_products((yh, yl), 2 * i, k + 1, right_w[k])
             for j in range(2):
                 p = 2 * i + j
                 applied = w0[k, p]
                 wave = vp[k, p]
                 residual = applied - corrs * wave
-                turned = (w1[k, p] + blocks[k][j] + value[BLK * k:BLK * (k + 1), BLK * j:BLK * (j + 1)]
+                turned = (w1[k, p] + rights[j] + ghosts[j] + value[BLK * k:BLK * (k + 1), BLK * j:BLK * (j + 1)]
                           - corrs * applied)
                 r0[k, p] = residual
                 w1[k, p] = turned
@@ -513,22 +551,20 @@
                 xh[p, BLK * (k + 1):BLK * (k + 2), :] = high
                 xl[p, BLK * (k + 1):BLK * (k + 2), :] = low
                 rr = rr + fold(residual * residual)
-                w0r = w0r + fold(applied * residual)
                 rt = rt + fold(residual * turned)
                 vt = vt + fold(wave * turned)
-                w0t = w0t + fold(applied * turned)
                 tt = tt + fold(turned * turned)
-        return rr, w0r, rt, vt, w0t, tt
+        return rr, rt, vt, tt
 
     def turned_down(part):
         at = pl.ds(2 * part, 2)
-        return remote(w1.at[0, at], t_ghost.at[0, at], send_t.at[0, part], recv_t.at[0, part], below)
+        return remote(w1.at[0, at], t_ghost.at[1, at], send_t.at[0, part], recv_t.at[0, part], below)
 
     def turned_up(part):
-        return remote(w1.at[1, pl.ds(PAIRS + 2 * part, 2)], t_ghost.at[1, pl.ds(2 * part, 2)],
+        return remote(w1.at[1, pl.ds(PAIRS + 2 * part, 2)], t_ghost.at[0, pl.ds(2 * part, 2)],
                       send_t.at[1, part], recv_t.at[1, part], above)
 
-    totals = (zeros,) * 6
+    totals = (zeros,) * 4
     for part in range(CHUNKS):
         totals = lax.fori_loop(0, 2, lambda n, c: finish(part + CHUNKS * n, c), totals)
 
@@ -539,90 +575,87 @@
         @pl.when(has_above)
         def _():
             turned_up(part).start()
-    w0t, tt = totals[4:]
-    spread(2, list(totals[:4]))
 
     def third_apply(i, total):
-        blocks = product_of((xh, xl), i, 1, 2, own_a, 0)
+        rhs = pair_of((xh,), i, 1, 2)[0]
+        value = dot(own_a[0], rhs) + dot(own_a[1], rhs)
         for k in range(2):
+            rights = right_products((xh,), 2 * i, k + 1, right_w[k, :BLK])
             for j in range(2):
-                total = total + fold(blocks[k][j] * w1[k, 2 * i + j])
+                p = 2 * i + j
+                both = 2.0 * w1[k, p] - xh[p, BLK * (k + 1):BLK * (k + 2), :].astype(F32)
+                image = value[BLK * k:BLK * (k + 1), BLK * j:BLK * (j + 1)] + rights[j]
+                total = total + fold(image * both)
         return total
 
     def third_phys(i, total):
+        at = pl.multiple_of(32 * i, 32)
         for k in range(2):
-            value = phys_piece(xh, xl, k, i)
-            at = pl.multiple_of(32 * i, 32)
+            rhs = phys_rows(xh, k, i)
+            value = dot(phys_a[0], rhs) + dot(phys_a[1], rhs)
             for p in range(PHYS):
                 rows = value[PHYS * p:PHYS * (p + 1)]
-                both = jnp.concatenate([rows[:, :BLK], rows[:, BLK:]], axis=0)
-                total = total + fold(both * w1[k, p, pl.ds(at, 32), :])
+                image = jnp.concatenate([rows[:, :BLK], rows[:, BLK:]], axis=0)
+                high = xh[p, pl.ds(pl.multiple_of(BLK * (k + 1) + 32 * i, 32), 32), :].astype(F32)
+                total = total + fold(image * (2.0 * w1[k, p, pl.ds(at, 32), :] - high))
         return total
 
     def cross(i, carry):
-        p = 2 * i
-        rhs = [jnp.concatenate([
-            jnp.concatenate([ref[p + j, 2 * BLK:3 * BLK, :], ref[p + PAIRS + j, BLK:2 * BLK, :]], axis=0)
-            for j in range(2)], axis=1) for ref in (xh, xl)]
-        value = split_dot((cross_a[0], cross_a[1]), rhs)
         for side in range(2):
+            blocks = packed_dot(cross_a[side], (xh, xl), 2 * i + PAIRS * (1 - side), side + 1)
             for j in range(2):
-                crossed[side, p + j] = value[BLK * side:BLK * (side + 1), BLK * j:BLK * (j + 1)]
+                crossed[side, 2 * i + j] = blocks[j]
         return carry
 
     lax.fori_loop(0, PAIRS // 2, cross, 0)
     tht = lax.fori_loop(0, PAIRS, third_apply, zeros)
     tht = lax.fori_loop(0, BLK // 32, third_phys, tht)
 
-    rr, w0r, rt, vt = collect(2, 4)
+    loads[5].wait()
+    masks = [(lax.broadcasted_iota(jnp.int32, (1, BLK), 1) < kept_ref[0, k]).astype(F32) for k in range(2)]
+
+    def masked(p, grams):
+        for k in range(2):
+            vectors = (vp[k, p], r0[k, p], w1[k, p])
+            pairs = [vectors[i] * vectors[j] for i in range(3) for j in range(i, 3)]
+            grams = tuple(gram + masks[k] * fold(pair) for gram, pair in zip(grams, pairs))
+        return grams
+
+    grams = lax.fori_loop(0, PHYS, masked, (zeros,) * 6)
+
+    for part in range(CHUNKS):
+        @pl.when(has_above)
+        def _():
+            turned_down(part).wait_recv()
+
+        @pl.when(has_below)
+        def _():
+            turned_up(part).wait_recv()
+
+    def meet(i, total):
+        return total + fold(crossed[0, i] * t_ghost[0, i]) + fold(crossed[1, i] * t_ghost[1, i])
+
+    tht = tht + 2.0 * lax.fori_loop(0, PAIRS, meet, zeros)
+    spread(2, list(totals) + [tht] + list(grams))
+    rr, rt, vt, tt, tht, mvv, mvr, mvt, mrr, mrt, mtt = collect(2, 11)
+    w0t = rt + corr * vt
     norm = jnp.sqrt(rr + EPS)
     curvature = rt / (rr + EPS)
-    coupled = w0r / norm
+    coupled = rr / norm
     ritz = 0.5 * (corr + curvature) - jnp.sqrt(0.25 * (corr - curvature) ** 2 + coupled * coupled)
     coef = ritz - corr
     magnitude = jnp.sqrt(coupled * coupled + coef * coef)
     wave_v = coupled / magnitude
     wave_r = coef / (magnitude * norm)
-    corr2 = wave_v * wave_v * corr + wave_v * wave_r * (vt + w0r) + wave_r * wave_r * rt
+    corr2 = wave_v * wave_v * corr + wave_v * wave_r * (vt + rr) + wave_r * wave_r * rt
     res_v = wave_v * (corr - corr2)
     res_r = wave_v - corr2 * wave_r
     res_t = wave_r
 
-    loads[5].wait()
-    masks = [(lax.broadcasted_iota(jnp.int32, (1, BLK), 1) < kept_ref[0, k]).astype(F32) for k in range(2)]
-    wide = [jnp.broadcast_to(value, (BLK, BLK)) for value in (wave_v, wave_r, wave_v * corr, res_v, res_r, res_t)]
-
-    def second_residual(p, totals):
-        rr2, ar2, mww, mwr, mrr = totals
-        for k in range(2):
-            wave, residual, turned = vp[k, p], r0[k, p], w1[k, p]
-            now = wide[0] * wave + wide[1] * residual
-            applied = wide[2] * wave + wide[0] * residual + wide[1] * turned
-            second = wide[3] * wave + wide[4] * residual + wide[5] * turned
-            rr2 = rr2 + fold(second * second)
-            ar2 = ar2 + fold(applied * second)
-            mww = mww + masks[k] * fold(now * now)
-            mwr = mwr + masks[k] * fold(now * second)
-            mrr = mrr + masks[k] * fold(second * second)
-        return rr2, ar2, mww, mwr, mrr
-
-    finals = lax.fori_loop(0, PHYS, second_residual, (zeros,) * 5)
-
-    for part in range(CHUNKS):
-        @pl.when(has_above)
-        def _():
-            turned_down(part).wait_recv()
-
-        @pl.when(has_below)
-        def _():
-            turned_up(part).wait_recv()
-
-    def meet(i, total):
-        return total + fold(crossed[0, i] * t_ghost[0, i]) + fold(crossed[1, i] * t_ghost[1, i])
-
-    tht = tht + 2.0 * lax.fori_loop(0, PAIRS, meet, zeros)
-    spread(3, list(finals) + [tht, w0t, tt])
-    rr2, ar2, mww, mwr, mrr, tht, w0t, tt = collect(3, 8)
+    rr2 = res_v * res_v + res_r * res_r * rr + res_t * res_t * tt + 2.0 * res_t * (res_v * vt + res_r * rt)
+    rr2 = jnp.maximum(rr2, 0.0)
+    wr2 = wave_v * res_v + wave_r * res_r * rr + res_t * (wave_v * vt + wave_r * rt)
+    ar2 = rr2 + corr2 * wr2
     norm2 = jnp.sqrt(rr2 + EPS)
     turned2 = (res_v * res_v * corr + res_r * res_r * rt + res_t * res_t * tht
                + 2.0 * (res_v * res_r * vt + res_v * res_t * w0t + res_r * res_t * tt))
@@ -633,19 +666,15 @@
     magnitude = jnp.sqrt(coupled * coupled + coef * coef)
     of_wave = coupled / magnitude
     of_res = coef / (magnitude * norm2)
-    kept = of_wave * of_wave * mww + 2.0 * of_wave * of_res * mwr + of_res * of_res * mrr
-    scale = 1.0 / jnp.sqrt(kept + EPS)
-    energy_ref[...] = jnp.broadcast_to(ritz, (8, BLK))
-    last = [jnp.broadcast_to(scale * value, (BLK, BLK)) for value in (
-        of_wave * wave_v + of_res * res_v, of_wave * wave_r + of_res * res_r, of_res * res_t)]
-
-    def write(p, carry):
-        for k in range(2):
-            value = last[0] * vp[k, p] + last[1] * r0[k, p] + last[2] * w1[k, p]
-            out_ref[k, p] = value * masks[k]
-        return carry
-
-    lax.fori_loop(0, PHYS, write, 0)
+    of_v = of_wave * wave_v + of_res * res_v
+    of_r = of_wave * wave_r + of_res * res_r
+    of_t = of_res * res_t
+    kept = (of_v * of_v * mvv + of_r * of_r * mrr + of_t * of_t * mtt
+            + 2.0 * (of_v * of_r * mvr + of_v * of_t * mvt + of_r * of_t * mrt))
+    scale = 1.0 / jnp.sqrt(jnp.maximum(kept, 0.0) + EPS)
+    last = [scale * value for value in (of_v, of_r, of_t)]
+    last_ref[...] = jnp.concatenate(
+        [jnp.broadcast_to(value, (1, BLK)) for value in last + [ritz]] + masks + [jnp.zeros((2, BLK), F32)], axis=0)
 
     for column in range(NX):
         @pl.when(x != column)
@@ -664,7 +693,7 @@
         @pl.when(my_slot != slot)
         def _():
             give(slot).wait_send()
-    for at in range(4):
+    for at in range(3):
         for hop in range(1, NS):
             remote(sums.at[at, sector], sums.at[at, sector], send_p.at[at, hop], recv_p.at[at, sector],
                    (chain, peer(hop))).wait_send()
@@ -673,33 +702,37 @@
     def _():
         coupling_up().wait_send()
         ghost_up().wait_send()
+        envs_up().wait_send()
         base_up().wait_send()
-        envs_up().wait_send()
         for part in range(CHUNKS):
             turned_up(part).wait_send()
 
     @pl.when(has_below)
     def _():
         ghost_down().wait_send()
+        envs_down().wait_send()
         base_down().wait_send()
-        envs_down().wait_send()
         for part in range(CHUNKS):
             turned_down(part).wait_send()
 
 
-def write_kernel(wave_ref, energy_in, left_in, out_ref, energy_ref, left_ref, rows, sem):
+def write_kernel(wave_ref, res_ref, turned_ref, last_ref, left_in, out_ref, energy_ref, left_ref, rows, sem):
     left_copy = pltpu.make_async_copy(left_in, left_ref, sem.at[8])
     left_copy.start()
-    energy_ref[0] = jnp.sum(energy_in[0:1, 0:1])
+    energy_ref[0] = jnp.sum(last_ref[3:4, 0:1])
+    size = ROWS // CHUNKS
+    count = size // PHYS
     copies = []
     for k in range(2):
+        mask = last_ref[4 + k:5 + k, :]
+        coefs = [jnp.broadcast_to(last_ref[i:i + 1, :] * mask, (count, BLK)) for i in range(3)]
         for part in range(CHUNKS):
-            size = ROWS // CHUNKS
+            at = pl.ds(count * part, count)
             for p in range(PHYS):
-                rows[k, pl.ds(size * part + p, size // PHYS, stride=PHYS), :] = (
-                    wave_ref[k, p, size // PHYS * part:size // PHYS * (part + 1), :])
-            at = pl.ds(size * part, size)
-            copies.append(pltpu.make_async_copy(rows.at[k, at], out_ref.at[k, at], sem.at[CHUNKS * k + part]))
+                rows[k, pl.ds(size * part + p, count, stride=PHYS), :] = (
+                    coefs[0] * wave_ref[k, p, at, :] + coefs[1] * res_ref[k, p, at, :] + coefs[2] * turned_ref[k, p, at, :])
+            to = pl.ds(size * part, size)
+            copies.append(pltpu.make_async_copy(rows.at[k, to], out_ref.at[k, to], sem.at[CHUNKS * k + part]))
             copies[-1].start()
     for copy in copies:
         copy.wait()
@@ -719,30 +752,31 @@
         return pltpu.VMEM((*lead, 2 * BLK, 2 * BLK), BF16)
 
     split_waves = pltpu.VMEM((PHYS, 4 * BLK, BLK), BF16)
-    wave, energy, left = pl.pallas_call(
+    waves = jax.ShapeDtypeStruct((2, PHYS, BLK, BLK), F32)
+    parts = pl.pallas_call(
         update_kernel,
         out_shape=(
-            jax.ShapeDtypeStruct((2, PHYS, BLK, BLK), F32),
+            waves, waves, waves,
             jax.ShapeDtypeStruct((8, BLK), F32),
             jax.ShapeDtypeStruct((2, BLK, BLK), F32),
         ),
         in_specs=[hbm] * 6,
-        out_specs=(vmem, vmem, vmem),
+        out_specs=(vmem,) * 5,
         scratch_shapes=[
             pltpu.VMEM((2, ROWS, BLK), F32), square(2), square(2), square(2), pltpu.VMEM((PHYS, PHYS), F32),
             pltpu.SMEM((1, 2), jnp.int32),
-            square(NX, 2), square(NX, 2), square(3, 2), square(3, 2), square(), square(2, PHYS), square(NX), square(NX),
-            pltpu.VMEM((2, ROWS, BLK), F32), square(), square(2, PHYS), square(2, PHYS), square(2, PHYS), square(2, PHYS),
-            square(2, PHYS), square(2, PAIRS), square(2, 2), square(2, PAIRS),
+            square(NX, 2), square(NX, 2), square(3, 2), square(3, 2), square(), square(2, PHYS), square(2, PHYS), square(NX), square(NX),
+            pltpu.VMEM((2, ROWS, BLK), F32), square(), square(2, PHYS), square(2, PHYS),
+            square(2, PAIRS), square(2, 2), square(2, PAIRS),
             split_waves, split_waves, split_waves, split_waves,
-            wide(2), wide(2), wide(2), wide(2), wide(2), wide(4), wide(2),
-            pltpu.VMEM((4, NS, 8, BLK), F32),
+            wide(4), wide(2), wide(2), wide(2), wide(4), wide(2),
+            pltpu.VMEM((3, NS, 16, BLK), F32),
             dma((6,)), dma((NX,)), dma((NX,)), dma((3, 2)), dma((3, 2)), dma((1,)), dma((1,)), dma((NX,)), dma((NX,)),
             dma((5,)), dma((5,)), dma((2,)), dma((2,)), dma((2, CHUNKS)), dma((2, CHUNKS)),
-            dma((4, NS)), dma((4, NS)),
+            dma((3, NS)), dma((3, NS)),
         ],
         compiler_params=pltpu.CompilerParams(
-            collective_id=0, has_side_effects=True, vmem_limit_bytes=50 << 20),
+            collective_id=0, has_side_effects=True, vmem_limit_bytes=36 << 20),
     )(*[pltpu.with_memory_space_constraint(value, pltpu.HBM) for value in (
         wave_start.reshape(2, ROWS, BLK), transfer[0], energy_terms[0], coupling[0], physical[0], kept_ranks)])
     out, energy, left = pl.pallas_call(
@@ -752,10 +786,11 @@
             jax.ShapeDtypeStruct((1,), F32),
             jax.ShapeDtypeStruct((2, BLK, BLK), F32),
         ),
-        in_specs=[vmem] * 3,
+        in_specs=[vmem] * 5,
         out_specs=(hbm, smem, hbm),
         scratch_shapes=[pltpu.VMEM((2, ROWS, BLK), F32), dma((9,))],
-    )(*[pltpu.with_memory_space_constraint(value, pltpu.VMEM) for value in (wave, energy, left)])
+        compiler_params=pltpu.CompilerParams(vmem_limit_bytes=16 << 20),
+    )(*[pltpu.with_memory_space_constraint(value, pltpu.VMEM) for value in parts])
     return (out.reshape(wave_start.shape), energy, left[None])
 
 

time: 71 us -> 65.1 us (0.917)
  Pallas kernels: 70.2 us -> 64.4 us
    pallas_call x1, Pallas kernels: 68 us -> 62.1 us  [per_device(): pl.pallas_call(update_kernel, out_shape=(waves, waves, waves, jax.ShapeDt...]
where the time goes in v4:
time: 65.1 us; the launch traced here: 65 us
  Pallas kernels  64.4 us (99%)
    pallas_call x1, Pallas kernels, per_device(): pl.pallas_call(update_kernel, out_shape=(waves, waves, waves, jax.ShapeDt...  62.1 us
    pallas_call x1, Pallas kernels, per_device(): pl.pallas_call(write_kernel, out_shape=(jax.ShapeDtypeStruct((2, ROWS, BL...  2.29 us

profile of v4, /device:TPU:1, one launch (start us, length us, event | category | flops | bytes accessed | tf_op | source)
XLA Modules:
  0.0 65.0 jit_solution(7529391989819792343)
XLA Ops:
  0.6 62.1 %shard_map.85 = (f32[2,16,128,128]{3,2,1,0:T(8,128)S(1)}, f32[2,16,128,128]{3,2,1,0:T(8,128)S(1)}, f32[2,16,128,128]{3,2,1,0:T(8,128)S(1)}, f32[8,128]{1,0:T(8,128)S(1)}, f32[2,128,128]{2,1,0:T(8,128)S(1)}) custom-call(f32[2,2048,128]{2,1,0:T(8,128)} %bitcast.7, f32[2,128,128]{2,1,0:T(8,128)} %bitcast.8, f32[2,128,128]{2,1,0:T(8,128)} %bitcast.9, ...), custom_call_target="tpu_custom_call" | custom-call | tf_op jit(solution)/shard_map/pallas_call | solution.py:756
  62.7 2.3 %shard_map.86 = (f32[2,2048,128]{2,1,0:T(8,128)}, f32[1]{0:T(128)}, f32[2,128,128]{2,1,0:T(8,128)}) custom-call(f32[2,16,128,128]{3,2,1,0:T(8,128)S(1)} %get-tuple-element.11.wave_ref, f32[2,16,128,128]{3,2,1,0:T(8,128)S(1)} %get-tuple-element.12.res_ref, f32[2,16,128,128]{3,2,1,0:T(8,128)S(1)} %get-tuple-element.13.turned_ref, ...), custom_call_target="tpu_custom_call" | custom-call | tf_op jit(solution)/shard_map/pallas_call | solution.py:782

commit v5 on v4

--- a/solution.py
+++ b/solution.py
@@ -400,16 +400,6 @@
     send_far(2)
     send(2, 0, product(qw, receive(1, 0)))
 
-    @pl.when(has_below)
-    def _():
-        ghost_up().wait_recv()
-
-    @pl.when(has_above)
-    def _():
-        ghost_down().wait_recv()
-
-    inverses = lax.fori_loop(0, PAIRS // 2, add_ghosts, inverses)
-
     @pl.when(zz >= 5)
     def _():
         remote(window.at[2, 1], far, send_f.at[0], recv_f.at[0], in_column(zz - 5)).wait_recv()
@@ -431,7 +421,15 @@
             def _():
                 give(slot).start()
     envs[pl.ds(x, 1)] = ends[pl.ds(my_slot, 1)]
-    lax.fori_loop(PAIRS // 2, PAIRS, add_ghosts, inverses)
+    @pl.when(has_below)
+    def _():
+        ghost_up().wait_recv()
+
+    @pl.when(has_above)
+    def _():
+        ghost_down().wait_recv()
+
+    lax.fori_loop(0, PAIRS, add_ghosts, inverses)
     lax.fori_loop(0, PAIRS, add_to_ghosts, 0)
     for column in range(NX):
         @pl.when(x != column)
@@ -607,9 +605,11 @@
                 crossed[side, 2 * i + j] = blocks[j]
         return carry
 
-    lax.fori_loop(0, PAIRS // 2, cross, 0)
-    tht = lax.fori_loop(0, PAIRS, third_apply, zeros)
-    tht = lax.fori_loop(0, BLK // 32, third_phys, tht)
+    def cross_and_phys(i, total):
+        cross(i, 0)
+        return third_phys(i, total)
+
+    tht = lax.fori_loop(0, PAIRS // 2, cross_and_phys, zeros)
 
     loads[5].wait()
     masks = [(lax.broadcasted_iota(jnp.int32, (1, BLK), 1) < kept_ref[0, k]).astype(F32) for k in range(2)]
@@ -621,7 +621,11 @@
             grams = tuple(gram + masks[k] * fold(pair) for gram, pair in zip(grams, pairs))
         return grams
 
-    grams = lax.fori_loop(0, PHYS, masked, (zeros,) * 6)
+    def apply_and_masked(i, carry):
+        total, grams = carry
+        return third_apply(i, total), masked(2 * i + 1, masked(2 * i, grams))
+
+    tht, grams = lax.fori_loop(0, PAIRS, apply_and_masked, (tht, (zeros,) * 6))
 
     for part in range(CHUNKS):
         @pl.when(has_above)

time: 65.1 us -> 64.5 us (level)
  no operation moved by 1% of the time
where the time goes in v5:
time: 64.5 us; the launch traced here: 64.4 us
  Pallas kernels  63.8 us (99%)
    pallas_call x1, Pallas kernels, per_device(): pl.pallas_call(update_kernel, out_shape=(waves, waves, waves, jax.ShapeDt...  61.5 us
    pallas_call x1, Pallas kernels, per_device(): pl.pallas_call(write_kernel, out_shape=(jax.ShapeDtypeStruct((2, ROWS, BL...  2.29 us

profile of v5, /device:TPU:1, one launch (start us, length us, event | category | flops | bytes accessed | tf_op | source)
XLA Modules:
  0.0 64.4 jit_solution(3575371949477791907)
XLA Ops:
  0.6 61.5 %shard_map.85 = (f32[2,16,128,128]{3,2,1,0:T(8,128)S(1)}, f32[2,16,128,128]{3,2,1,0:T(8,128)S(1)}, f32[2,16,128,128]{3,2,1,0:T(8,128)S(1)}, f32[8,128]{1,0:T(8,128)S(1)}, f32[2,128,128]{2,1,0:T(8,128)S(1)}) custom-call(f32[2,2048,128]{2,1,0:T(8,128)} %bitcast.7, f32[2,128,128]{2,1,0:T(8,128)} %bitcast.8, f32[2,128,128]{2,1,0:T(8,128)} %bitcast.9, ...), custom_call_target="tpu_custom_call" | custom-call | tf_op jit(solution)/shard_map/pallas_call | solution.py:760
  62.1 2.3 %shard_map.86 = (f32[2,2048,128]{2,1,0:T(8,128)}, f32[1]{0:T(128)}, f32[2,128,128]{2,1,0:T(8,128)}) custom-call(f32[2,16,128,128]{3,2,1,0:T(8,128)S(1)} %get-tuple-element.11.wave_ref, f32[2,16,128,128]{3,2,1,0:T(8,128)S(1)} %get-tuple-element.12.res_ref, f32[2,16,128,128]{3,2,1,0:T(8,128)S(1)} %get-tuple-element.13.turned_ref, ...), custom_call_target="tpu_custom_call" | custom-call | tf_op jit(solution)/shard_map/pallas_call | solution.py:786

commit v6 on v5

--- a/solution.py
+++ b/solution.py
@@ -207,19 +207,24 @@
         t_ghost[1] = jnp.zeros((PAIRS, BLK, BLK), F32)
         lr_ghost[1] = jnp.zeros((2, BLK, BLK), F32)
 
+    for column in range(NX):
+        @pl.when(x != column)
+        def _():
+            deal(column).wait_send()
+
+    @pl.when(has_above)
+    def _():
+        ghost_up().start()
+
+    @pl.when(has_below)
+    def _():
+        ghost_down().start()
+
     for slot in range(NX):
         @pl.when(my_slot != slot)
         def _():
             remote(mine.at[slot], elements.at[slot], send_a.at[slot], recv_a.at[slot],
                    in_row(lax.rem(x + 1, NX))).wait_recv()
-
-    @pl.when(has_above)
-    def _():
-        ghost_up().start()
-
-    @pl.when(has_below)
-    def _():
-        ghost_down().start()
 
     q0, q1, q2, q3 = [elements[s, 0] for s in range(NX)]
     s0, s1, s2, s3 = [elements[s, 1] for s in range(NX)]
@@ -680,10 +685,6 @@
     last_ref[...] = jnp.concatenate(
         [jnp.broadcast_to(value, (1, BLK)) for value in last + [ritz]] + masks + [jnp.zeros((2, BLK), F32)], axis=0)
 
-    for column in range(NX):
-        @pl.when(x != column)
-        def _():
-            deal(column).wait_send()
     for at in range(3):
         for part in range(2):
             @pl.when(sends[at][part])

time: 64.5 us -> 62.3 us (0.966)
  Pallas kernels: 63.8 us -> 61.5 us
    pallas_call x1, Pallas kernels: 61.5 us -> 59.2 us  [per_device(): pl.pallas_call(update_kernel, out_shape=(waves, waves, waves, jax.ShapeDt...]
where the time goes in v6:
time: 62.3 us; the launch traced here: 62.2 us
  Pallas kernels  61.5 us (99%)
  between operations  0.64 us (1%)
    pallas_call x1, Pallas kernels, per_device(): pl.pallas_call(update_kernel, out_shape=(waves, waves, waves, jax.ShapeDt...  59.2 us
    pallas_call x1, Pallas kernels, per_device(): pl.pallas_call(write_kernel, out_shape=(jax.ShapeDtypeStruct((2, ROWS, BL...  2.29 us

profile of v6, /device:TPU:1, one launch (start us, length us, event | category | flops | bytes accessed | tf_op | source)
XLA Modules:
  0.0 62.2 jit_solution(17966224568798192471)
XLA Ops:
  0.6 59.2 %shard_map.85 = (f32[2,16,128,128]{3,2,1,0:T(8,128)S(1)}, f32[2,16,128,128]{3,2,1,0:T(8,128)S(1)}, f32[2,16,128,128]{3,2,1,0:T(8,128)S(1)}, f32[8,128]{1,0:T(8,128)S(1)}, f32[2,128,128]{2,1,0:T(8,128)S(1)}) custom-call(f32[2,2048,128]{2,1,0:T(8,128)} %bitcast.7, f32[2,128,128]{2,1,0:T(8,128)} %bitcast.8, f32[2,128,128]{2,1,0:T(8,128)} %bitcast.9, ...), custom_call_target="tpu_custom_call" | custom-call | tf_op jit(solution)/shard_map/pallas_call | solution.py:761
  59.9 2.3 %shard_map.86 = (f32[2,2048,128]{2,1,0:T(8,128)}, f32[1]{0:T(128)}, f32[2,128,128]{2,1,0:T(8,128)}) custom-call(f32[2,16,128,128]{3,2,1,0:T(8,128)S(1)} %get-tuple-element.11.wave_ref, f32[2,16,128,128]{3,2,1,0:T(8,128)S(1)} %get-tuple-element.12.res_ref, f32[2,16,128,128]{3,2,1,0:T(8,128)S(1)} %get-tuple-element.13.turned_ref, ...), custom_call_target="tpu_custom_call" | custom-call | tf_op jit(solution)/shard_map/pallas_call | solution.py:787

commit v7 on v6

--- a/solution.py
+++ b/solution.py
@@ -405,6 +405,8 @@
     send_far(2)
     send(2, 0, product(qw, receive(1, 0)))
 
+    lax.fori_loop(0, PAIRS, add_to_ghosts, 0)
+
     @pl.when(zz >= 5)
     def _():
         remote(window.at[2, 1], far, send_f.at[0], recv_f.at[0], in_column(zz - 5)).wait_recv()
@@ -435,7 +437,6 @@
         ghost_down().wait_recv()
 
     lax.fori_loop(0, PAIRS, add_ghosts, inverses)
-    lax.fori_loop(0, PAIRS, add_to_ghosts, 0)
     for column in range(NX):
         @pl.when(x != column)
         def _():

time: 62.3 us -> 62.3 us (level)
  no operation moved by 1% of the time
where the time goes in v7:
time: 62.3 us; the launch traced here: 62.2 us
  Pallas kernels  61.5 us (99%)
  between operations  0.64 us (1%)
    pallas_call x1, Pallas kernels, per_device(): pl.pallas_call(update_kernel, out_shape=(waves, waves, waves, jax.ShapeDt...  59.2 us
    pallas_call x1, Pallas kernels, per_device(): pl.pallas_call(write_kernel, out_shape=(jax.ShapeDtypeStruct((2, ROWS, BL...  2.29 us

profile of v7, /device:TPU:1, one launch (start us, length us, event | category | flops | bytes accessed | tf_op | source)
XLA Modules:
  0.0 62.2 jit_solution(5486808716784261767)
XLA Ops:
  0.6 59.2 %shard_map.85 = (f32[2,16,128,128]{3,2,1,0:T(8,128)S(1)}, f32[2,16,128,128]{3,2,1,0:T(8,128)S(1)}, f32[2,16,128,128]{3,2,1,0:T(8,128)S(1)}, f32[8,128]{1,0:T(8,128)S(1)}, f32[2,128,128]{2,1,0:T(8,128)S(1)}) custom-call(f32[2,2048,128]{2,1,0:T(8,128)} %bitcast.7, f32[2,128,128]{2,1,0:T(8,128)} %bitcast.8, f32[2,128,128]{2,1,0:T(8,128)} %bitcast.9, ...), custom_call_target="tpu_custom_call" | custom-call | tf_op jit(solution)/shard_map/pallas_call | solution.py:762
  59.9 2.3 %shard_map.86 = (f32[2,2048,128]{2,1,0:T(8,128)}, f32[1]{0:T(128)}, f32[2,128,128]{2,1,0:T(8,128)}) custom-call(f32[2,16,128,128]{3,2,1,0:T(8,128)S(1)} %get-tuple-element.11.wave_ref, f32[2,16,128,128]{3,2,1,0:T(8,128)S(1)} %get-tuple-element.12.res_ref, f32[2,16,128,128]{3,2,1,0:T(8,128)S(1)} %get-tuple-element.13.turned_ref, ...), custom_call_target="tpu_custom_call" | custom-call | tf_op jit(solution)/shard_map/pallas_call | solution.py:788
